TPU v7x, 768 devices: a whole 4x8x12 slice. The times are simulated.
768 devices in a mesh: team: 128 (over x, z_lo, y), rep: 6 (over z_hi, core).
Axes of the slice: x: 4, y: 8, z: 12 (z_hi: 3, z_lo: 4; z = z_hi * 4 + z_lo), core: 2. Of those that a mesh axis runs over, the one named last changes fastest.
Arguments:
- features: bfloat16 [147456, 128], P('team'), may hold values from -6 to 6
- degrees: int32 [147456], P('team'), may hold values from 1 to 16
- tiles: bfloat16 [6, 147456, 1152], P('rep', 'team'), may hold values from -0.15625 to 0.15625
- pattern: int32 [6, 128], P('rep', 'team'), may hold values 0 or 1
- weight: bfloat16 [128, 256], replicated, may hold values from -0.5 to 0.5
- cotangent: bfloat16 [147456, 256], P('team'), may hold values from -6 to 6
Outputs:
- hidden: bfloat16 [147456, 256], P(('team', 'rep'))
- grad_features: bfloat16 [147456, 128], P(('team', 'rep'))
- grad_weight: float32 [128, 256], replicated
All inputs are finite; a program needn't handle non-finite values. No bound on the sum of `pattern` on one device may be relied on, other than what follows from the above.
Results may differ from a plain program's by a relative error of at most 0.006.
Values may be sent and summed in bfloat16 or wider, within the bound.
No kernel may reach another device: no remote copies, remote signals or barrier semaphores. Data moves between devices by JAX's collectives and lax.ppermute only.
A program may use at most 32 MiB of HBM per device.

v0:
```python
import math

import jax
import jax.numpy as jnp
from jax import lax
from jax.sharding import PartitionSpec as P


def shifted(block, axis, distance):
    devices = range(lax.axis_size(axis))
    route = [((i - distance) % len(devices), i) for i in devices]
    return lax.ppermute(block, axis, route)


def silu_grad(value):
    sig = jax.nn.sigmoid(value)
    return sig * (1.0 + value * (1.0 - sig))


def local(features, degrees, tiles, pattern, weight, cotangent):
    team_count = lax.axis_size("team")
    stop_count = lax.axis_size("rep")
    rep_index = lax.axis_index("rep")
    row_count = features.shape[0]
    own_rows = row_count // stop_count
    row_start = rep_index * own_rows
    inv_root = 1.0 / jnp.sqrt(degrees.astype(jnp.float32))
    inv_own = lax.dynamic_slice_in_dim(inv_root, row_start, own_rows, 0)
    source = (features.astype(jnp.float32) * inv_root[:, None]).astype(jnp.bfloat16)
    tile_on = pattern[0, 0].astype(jnp.float32)
    tile_now = tiles[0]
    passing = source
    own_block = source
    for stop_num in range(1, stop_count):
        passing = shifted(passing, "team", 1)
        own_block = jnp.where(rep_index == stop_num, passing, own_block)
    partial_value = jnp.dot(tile_now, own_block, preferred_element_type=jnp.float32) * tile_on
    grad_scale = 1.0 / math.sqrt(row_count * team_count)
    totals = lax.psum(partial_value, "rep")
    aggregated = (totals * inv_root[:, None]).astype(jnp.bfloat16)
    pre_act = jnp.dot(aggregated, weight, preferred_element_type=jnp.float32)
    hidden_full = jax.nn.silu(pre_act).astype(jnp.bfloat16)
    hidden = lax.dynamic_slice_in_dim(hidden_full, row_start, own_rows, 0)
    slope_term = (cotangent.astype(jnp.float32) * silu_grad(pre_act)).astype(jnp.bfloat16)
    grad_local = lax.dot_general(
        aggregated, slope_term, (((0,), (0,)), ((), ())), preferred_element_type=jnp.float32
    )
    grad_weight = lax.psum(grad_local, "team") * grad_scale
    message = (
        lax.dot_general(
            slope_term, weight, (((1,), (1,)), ((), ())), preferred_element_type=jnp.float32
        )
        * inv_root[:, None]
    ).astype(jnp.bfloat16)
    back_term = (
        lax.dot_general(
            tile_now, message, (((0,), (0,)), ((), ())), preferred_element_type=jnp.float32
        )
        * tile_on
    )
    carried = jnp.zeros_like(back_term)
    for stop_num in reversed(range(stop_count)):
        carried = carried + jnp.where(rep_index == stop_num, back_term, 0.0)
        if stop_num > 0:
            carried = shifted(carried, "team", -1)
    summed = lax.psum_scatter(carried, "rep", scatter_dimension=0, tiled=True)
    grad_features = (summed * inv_own[:, None]).astype(jnp.bfloat16)
    return (hidden, grad_features, grad_weight)


def solution(mesh):
    in_specs = (
        P("team", None),
        P("team"),
        P("rep", "team", None),
        P("rep", "team"),
        P(),
        P("team", None),
    )
    out_specs = (P(("team", "rep"), None), P(("team", "rep"), None), P())
    return jax.shard_map(local, mesh=mesh, in_specs=in_specs, out_specs=out_specs, check_vma=False)
```

profile of v0, /device:TPU:1, one launch (start us, length us, event | category | flops | bytes accessed | tf_op | source)
XLA Modules:
  0.0 1555.1 jit_solution(16949526319607957207)
XLA Ops:
  7.2 0.0 all-reduce.3.cloned.1.call-start
  7.2 1.3 copy.11
  8.5 0.7 convert_rsqrt_fusion
  9.2 0.1 multiply_convert_fusion.2
  9.3 4.0 collective-permute-start
  13.3 13.6 collective-permute-done
  27.0 1.9 collective-permute-start.1
  28.9 11.6 collective-permute-done.1
  40.4 1.9 collective-permute-start.2
  42.3 11.6 collective-permute-done.2
  53.9 0.7 copy-done.1
  54.6 1.9 collective-permute-start.3
  56.5 11.7 collective-permute-done.3
  68.2 1.9 collective-permute-start.4
  70.8 11.2 collective-permute-done.4
  82.0 1.8 fusion.10
  83.8 0.0 all-reduce.3.cloned.1.call-update
  83.8 0.0 all-reduce.5.cloned.1.call-start
  83.9 92.3 %all-reduce.3.cloned.1.call-done = f32[1152,128]{0,1:T(8,128)} async-done(((f32[1152,128]{0,1:T(8,128)}), f32[1152,128]{0,1:T(8,128)}) %all-reduce.3.cloned.1.call-update) | async-done | bytes 589840 | tf_op jit(solution)/shard_map/psum | solution.py:39
  176.2 3.4 multiply_convert_fusion
  179.6 1.8 fusion.7
  181.5 9.9 collective-permute-start.5
  191.4 12.6 collective-permute-done.5
  204.0 0.1 bitcast_add_fusion.4
  204.1 9.8 collective-permute-start.6
  213.9 12.5 collective-permute-done.6
  226.4 0.1 bitcast_add_fusion.3
  226.5 10.1 collective-permute-start.7
  236.6 11.6 collective-permute-done.7
  248.2 0.1 bitcast_add_fusion.2
  248.3 10.1 collective-permute-start.8
  258.4 10.7 collective-permute-done.8
  269.1 0.9 bitcast_add_fusion.1
  269.9 10.1 collective-permute-start.9
  280.1 2.2 fusion.26
  282.2 0.0 all-reduce.5.cloned.1.call-update
  282.3 0.0 reduce-scatter.4.cloned.1.call-start
  282.3 7.9 collective-permute-done.9
  290.2 1.9 bitcast_add_fusion
  292.1 2.1 copy.13
  294.2 0.0 reduce-scatter.4.cloned.1.call-update
  294.3 0.1 dynamic_slice.7
  294.3 1.7 fusion.25
  296.0 1179.5 %all-reduce.5.cloned.1.call-done = f32[128,256]{1,0:T(8,128)} async-done(((f32[128,256]{1,0:T(8,128)}), f32[128,256]{1,0:T(8,128)}) %all-reduce.5.cloned.1.call-update) | async-done | bytes 131088 | tf_op jit(solution)/shard_map/psum | solution.py:48
  1475.6 1.6 broadcast_multiply_fusion
  1477.1 69.7 %reduce-scatter.4.cloned.1.call-done = f32[192,128]{1,0:T(8,128)} async-done(((f32[1152,128]{1,0:T(8,128)}), f32[192,128]{1,0:T(8,128)}) %reduce-scatter.4.cloned.1.call-update) | async-done | bytes 98320
  1546.8 1.0 copy.14
  1547.9 0.7 copy.12
  (7 shorter events, 0.1 us)
Async XLA Ops:
  7.2 74.8 %copy-start = (bf16[1,1152,1152]{2,1,0:T(8,128)(2,1)S(1)}, bf16[1,1152,1152]{2,1,0:T(8,128)(2,1)}, u32[]{:S(2)}) copy-start(bf16[1,1152,1152]{2,1,0:T(8,128)(2,1)} %param.8) | copy-start | bytes 7962628
  7.2 169.0 %all-reduce.3.cloned.1.call-start = ((), (), s32[]{:S(2)}) async-start(), calls=%async_computation.1 | async-start | bytes 1179648 | tf_op jit(solution)/shard_map/psum | solution.py:39
  9.3 17.7 %collective-permute-start = (bf16[1152,128]{0,1:T(8,128)(2,1)S(1)}, bf16[1152,128]{0,1:T(8,128)(2,1)S(1)}, u32[]{:S(2)}, u32[]{:S(2)}) collective-permute-start(bf16[1152,128]{0,1:T(8,128)(2,1)S(1)} %multiply_convert_fusion.2), channel_id=1, source_target_pairs={{762,0},{0,6},{6,12},{12,18},{18,24},{24,30},{30,36},{36,42},{42,4... | collective-permute-start | bytes 884744 | tf_op jit(solution)/shard_map/ppermute | solution.py:12
  27.0 13.5 collective-permute-start.1
  40.4 13.5 collective-permute-start.2
  53.9 0.7 copy-start.1
  54.6 13.6 collective-permute-start.3
  68.2 13.8 collective-permute-start.4
  83.8 95.8 %copy-start.2 = (bf16[128,256]{1,0:T(8,128)(2,1)S(1)}, bf16[128,256]{1,0:T(8,128)(2,1)}, u32[]{:S(2)}) copy-start(bf16[128,256]{1,0:T(8,128)(2,1)} %param.10) | copy-start | bytes 196612
  83.8 1391.8 %all-reduce.5.cloned.1.call-start = ((), (), s32[]{:S(2)}) async-start(), calls=%async_computation.2 | async-start | bytes 262144 | tf_op jit(solution)/shard_map/psum | solution.py:48
  181.5 22.5 %collective-permute-start.5 = (f32[1152,128]{0,1:T(8,128)S(1)}, f32[1152,128]{0,1:T(8,128)S(1)}, u32[]{:S(2)}, u32[]{:S(2)}) collective-permute-start(f32[1152,128]{0,1:T(8,128)S(1)} %select_bitcast_fusion), channel_id=1, source_target_pairs={{6,0},{12,6},{18,12},{24,18},{30,24},{36,30},{42,36},{48,42},{54,4... | collective-permute-start | bytes 1769480 | tf_op jit(solution)/shard_map/ppermute | solution.py:12
  204.1 22.3 %collective-permute-start.6 = (f32[1152,128]{0,1:T(8,128)S(1)}, f32[1152,128]{0,1:T(8,128)S(1)}, u32[]{:S(2)}, u32[]{:S(2)}) collective-permute-start(f32[1152,128]{0,1:T(8,128)S(1)} %bitcast_add_fusion.4), channel_id=1, source_target_pairs={{6,0},{12,6},{18,12},{24,18},{30,24},{36,30},{42,36},{48,42},{54,4... | collective-permute-start | bytes 1769480 | tf_op jit(solution)/shard_map/ppermute | solution.py:12
  226.5 21.7 %collective-permute-start.7 = (f32[1152,128]{0,1:T(8,128)S(1)}, f32[1152,128]{0,1:T(8,128)S(1)}, u32[]{:S(2)}, u32[]{:S(2)}) collective-permute-start(f32[1152,128]{0,1:T(8,128)S(1)} %bitcast_add_fusion.3), channel_id=1, source_target_pairs={{6,0},{12,6},{18,12},{24,18},{30,24},{36,30},{42,36},{48,42},{54,4... | collective-permute-start | bytes 1769480 | tf_op jit(solution)/shard_map/ppermute | solution.py:12
  248.3 20.8 %collective-permute-start.8 = (f32[1152,128]{0,1:T(8,128)S(1)}, f32[1152,128]{0,1:T(8,128)S(1)}, u32[]{:S(2)}, u32[]{:S(2)}) collective-permute-start(f32[1152,128]{0,1:T(8,128)S(1)} %bitcast_add_fusion.2), channel_id=1, source_target_pairs={{6,0},{12,6},{18,12},{24,18},{30,24},{36,30},{42,36},{48,42},{54,4... | collective-permute-start | bytes 1769480 | tf_op jit(solution)/shard_map/ppermute | solution.py:12
  269.9 20.2 %collective-permute-start.9 = (f32[1152,128]{0,1:T(8,128)}, f32[1152,128]{0,1:T(8,128)}, u32[]{:S(2)}, u32[]{:S(2)}) collective-permute-start(f32[1152,128]{0,1:T(8,128)} %bitcast_add_fusion.1), channel_id=1, source_target_pairs={{6,0},{12,6},{18,12},{24,18},{30,24},{36,30},{42,36},{48,42},{54,4... | collective-permute-start | bytes 1769480 | tf_op jit(solution)/shard_map/ppermute | solution.py:12
  282.3 1264.6 %reduce-scatter.4.cloned.1.call-start = ((), (), s32[]{:S(2)}) async-start(), calls=%async_computation.3 | async-start | bytes 688128
Sparse Core Ops, SparseCore 0:
  83.9 92.2 all-reduce.2
  282.4 1193.1 all-reduce.4
  1478.7 68.0 reduce-scatter.3
where the time goes:
time: 1560 us
  waiting for transfers between devices  1460 us (94%)
  starting transfers between devices  61.9 us (4%)
    psum x1, waiting for transfers between devices, local(): grad_weight = lax.psum(grad_local, 'team') * grad_scale  1180 us
    ppermute x10, waiting for transfers between devices, shifted(): return lax.ppermute(block, axis, route)  115 us
    psum x1, waiting for transfers between devices, local(): totals = lax.psum(partial_value, 'rep')  92.3 us
    unnamed x4, waiting for transfers between devices  69.8 us
    ppermute x10, starting transfers between devices, shifted(): return lax.ppermute(block, axis, route)  61.8 us
  transfers between devices with their start and end apart: 13, of which 13 were waited for; matrix products, arithmetic and copies ran while one was open for 1% of the time, Pallas kernels for 0%

commit v1 on v0

v1 whole, which is shorter than its diff:
```python
import math

import jax
import jax.numpy as jnp
from jax import lax
from jax.sharding import PartitionSpec as P

BF = jnp.bfloat16
F32 = jnp.float32


def local(features, degrees, tiles, pattern, weight, cotangent):
    teams = lax.axis_size("team")
    reps = lax.axis_size("rep")
    zs = reps // 2
    rep = lax.axis_index("rep")
    z, core = rep // 2, rep % 2
    rows, feat = features.shape
    hid = weight.shape[1]
    own = rows // reps
    half = zs * own

    def across(value, move):
        route = [(i * reps + s, (move(i, s)[0] % teams) * reps + move(i, s)[1]) for i in range(teams) for s in range(reps)]
        return lax.ppermute(value, ("team", "rep"), route)

    def swap_core(value):
        return lax.ppermute(value, "rep", [(s, s ^ 1) for s in range(reps)])

    def pick(array, which):
        return lax.dynamic_index_in_dim(array, which, 1, keepdims=False)

    inv_root = 1.0 / jnp.sqrt(degrees.astype(F32))
    inv_half = pick(inv_root.reshape(zs, 2, own), core).reshape(half)
    inv_own = lax.dynamic_slice_in_dim(inv_root, rep * own, own, 0)
    source = (features.astype(F32) * inv_root[:, None]).astype(BF)
    tile_on = pattern[0, 0].astype(F32)
    tile = tiles[0]

    block = across(source, lambda i, s: (i + s, s))
    partial = jnp.dot(tile, block, preferred_element_type=F32) * tile_on
    parts = partial.reshape(zs, 2, own, feat)

    chip = pick(parts, core) + swap_core(pick(parts, 1 - core).astype(BF)).astype(F32)
    sent = chip.astype(BF)
    from1 = lax.ppermute(sent, "rep", [(s, (s + 2) % reps) for s in range(reps)])
    from2 = lax.ppermute(sent, "rep", [(s, (s + 4) % reps) for s in range(reps)])
    first = jnp.where(z == 0, sent, jnp.where(z == 1, from1, from2)).astype(F32)
    second = jnp.where(z == 1, sent, jnp.where(z == 2, from1, from2)).astype(F32)
    third = jnp.where(z == 2, sent, jnp.where(z == 0, from1, from2)).astype(F32)
    totals = (first + second + third).reshape(half, feat)

    aggregated = (totals * inv_half[:, None]).astype(BF)
    pre_act = jnp.dot(aggregated, weight, preferred_element_type=F32)
    sig = jax.nn.sigmoid(pre_act)
    hidden_half = (pre_act * sig).astype(BF)
    hidden = lax.dynamic_slice_in_dim(hidden_half, z * own, own, 0)
    cot_half = pick(cotangent.reshape(zs, 2, own, hid), core).reshape(half, hid)
    slope = (cot_half.astype(F32) * (sig * (1.0 + pre_act * (1.0 - sig)))).astype(BF)
    grad_part = lax.dot_general(aggregated, slope, (((0,), (0,)), ((), ())), preferred_element_type=F32)
    message_half = (
        lax.dot_general(slope, weight, (((1,), (1,)), ((), ())), preferred_element_type=F32) * inv_half[:, None]
    ).astype(BF)

    message_other = swap_core(message_half)
    mine, other = message_half.reshape(zs, 1, own, feat), message_other.reshape(zs, 1, own, feat)
    even, odd = jnp.where(core == 0, mine, other), jnp.where(core == 0, other, mine)
    message = jnp.concatenate([even, odd], axis=1).reshape(rows, feat)

    grad_parts = grad_part.reshape(2, feat // 2, hid)
    grad = lax.dynamic_index_in_dim(grad_parts, core, 0, keepdims=False) + swap_core(
        lax.dynamic_index_in_dim(grad_parts, 1 - core, 0, keepdims=False)
    )
    bit = 1
    while bit < teams:
        grad = grad + lax.ppermute(grad, "team", [(i, i ^ bit) for i in range(teams)])
        bit *= 2
    grad = grad * (1.0 / math.sqrt(rows * teams))
    grad_other = swap_core(grad)
    grad_weight = jnp.concatenate(
        [jnp.where(core == 0, grad, grad_other), jnp.where(core == 0, grad_other, grad)], axis=0
    )

    back = lax.dot_general(tile, message, (((0,), (0,)), ((), ())), preferred_element_type=F32) * tile_on
    backs = back.reshape(zs, 2, own, feat)
    pair = pick(backs, core) + across(
        pick(backs, 1 - core).astype(BF), lambda i, s: (i + 1 if s % 2 == 0 else i - 1, s ^ 1)
    ).astype(F32)
    sent = pair.astype(BF)
    summed = 0.0
    for k in range(zs):
        chunk = lax.dynamic_index_in_dim(sent, (z + k) % zs, 0, keepdims=False)
        summed = summed + across(chunk, lambda i, s: (i - s, 2 * ((s // 2 + k) % zs) + s % 2)).astype(F32)
    grad_features = (summed * inv_own[:, None]).astype(BF)
    return (hidden, grad_features, grad_weight)


def solution(mesh):
    in_specs = (
        P("team", None),
        P("team"),
        P("rep", "team", None),
        P("rep", "team"),
        P(),
        P("team", None),
    )
    out_specs = (P(("team", "rep"), None), P(("team", "rep"), None), P())
    return jax.shard_map(local, mesh=mesh, in_specs=in_specs, out_specs=out_specs, check_vma=False)
```

time: 1560 us -> 148 us (0.09)
  waiting for transfers between devices: 1460 us -> 40.7 us
  starting transfers between devices: 61.9 us -> 85.9 us
    psum x2 -> x0, waiting for transfers between devices: 1270 us -> none  [the longest x1 1180 us: local(): grad_weight = lax.psum(grad_local, 'team') * grad_scale]
    ppermute x10 -> x18, waiting for transfers between devices: 115 us -> 40.7 us  [the longest x5 14.3 us: across(): return lax.ppermute(value, ('team', 'rep'), route)]
    unnamed x4 -> x0, waiting for transfers between devices: 69.8 us -> none
    ppermute x10 -> x18, starting transfers between devices: 61.8 us -> 85.9 us  [the longest x5 29.8 us: across(): return lax.ppermute(value, ('team', 'rep'), route)]
  transfers between devices with their start and end apart: 13 -> 18, of which waited for: 13 -> 10; matrix products, arithmetic and copies ran while one was open for 1% -> 6% of each run, Pallas kernels for 0% -> 0%
where the time goes in v1:
time: 148 us; the launch traced here: 147 us
  starting transfers between devices  85.9 us (58%)
  waiting for transfers between devices  40.7 us (28%)
  other arithmetic  7.49 us (5%)
  local copies, waits for them, and re-layouts  6.26 us (4%)
  matrix products  5.02 us (3%)
  between operations  1.79 us (1%)
    ppermute x5, starting transfers between devices, across(): return lax.ppermute(value, ('team', 'rep'), route)  29.8 us
    ppermute x1, starting transfers between devices, local(): lax.ppermute(sent, 'rep', [(s, (s + 2) % reps) for s in range(reps)])  23.3 us
    ppermute x7, starting transfers between devices, local(): lax.ppermute(grad, 'team', [(i, i ^ bit) for i in range(teams)])  21.1 us
    ppermute x5, waiting for transfers between devices, across(): return lax.ppermute(value, ('team', 'rep'), route)  14.3 us
    ppermute x7, waiting for transfers between devices, local(): lax.ppermute(grad, 'team', [(i, i ^ bit) for i in range(teams)])  11.2 us
    ppermute x4, starting transfers between devices, swap_core(): return lax.ppermute(value, 'rep', [(s, s ^ 1) for s in range(reps)])  8.17 us
    ppermute x1, waiting for transfers between devices, local(): lax.ppermute(sent, 'rep', [(s, (s + 4) % reps) for s in range(reps)])  7.73 us
    ppermute x1, waiting for transfers between devices, local(): lax.ppermute(sent, 'rep', [(s, (s + 2) % reps) for s in range(reps)])  6.11 us
  transfers between devices with their start and end apart: 18, of which 10 were waited for; matrix products, arithmetic and copies ran while one was open for 6% of the time, Pallas kernels for 0%

profile of v1, /device:TPU:1, one launch (start us, length us, event | category | flops | bytes accessed | tf_op | source)
XLA Modules:
  0.0 147.1 jit_solution(7479025686836958744)
XLA Ops:
  0.6 0.9 convert_rsqrt_fusion
  1.5 1.2 multiply_convert_fusion
  2.7 4.0 %collective-permute-start = (bf16[1152,128]{1,0:T(8,128)(2,1)S(1)}, bf16[1152,128]{1,0:T(8,128)(2,1)S(1)}, u32[]{:S(2)}, u32[]{:S(2)}) collective-permute-start(bf16[1152,128]{1,0:T(8,128)(2,1)S(1)} %multiply_convert_fusion), channel_id=1, source_target_pairs={{0,0},{1,7},{2,14},{3,21},{4,28},{5,35},{6,6},{7,13},{8,20},{9,27}... | collective-permute-start | bytes 884744 | tf_op jit(solution)/shard_map/ppermute | solution.py:25
  7.4 12.9 %collective-permute-done = bf16[1152,128]{1,0:T(8,128)(2,1)S(1)} collective-permute-done((bf16[1152,128]{1,0:T(8,128)(2,1)S(1)}, bf16[1152,128]{1,0:T(8,128)(2,1)S(1)}, u32[]{:S(2)}, u32[]{:S(2)}) %collective-permute-start) | collective-permute-done | bytes 294944 | tf_op jit(solution)/shard_map/ppermute | solution.py:25
  20.3 0.9 fusion.13
  21.3 1.1 copy.15
  22.4 1.0 fusion.24
  23.3 1.9 %collective-permute-start.1 = (bf16[3,192,128]{2,1,0:T(8,128)(2,1)S(1)}, bf16[3,192,128]{2,1,0:T(8,128)(2,1)S(1)}, u32[]{:S(2)}, u32[]{:S(2)}) collective-permute-start(bf16[3,192,128]{2,1,0:T(8,128)(2,1)S(1)} %fusion.24), channel_id=1, source_target_pairs={{0,1},{1,0},{2,3},{3,2},{4,5},{5,4},{6,7},{7,6},{8,9},{9,8},{10,11... | collective-permute-start | bytes 442376 | tf_op jit(solution)/shard_map/ppermute | solution.py:28
  25.3 1.3 collective-permute-done.1
  26.6 1.0 fusion.22
  27.6 23.3 %collective-permute-start.2 = (bf16[3,192,128]{2,1,0:T(8,128)(2,1)S(1)}, bf16[3,192,128]{2,1,0:T(8,128)(2,1)S(1)}, u32[]{:S(2)}, u32[]{:S(2)}) collective-permute-start(bf16[3,192,128]{2,1,0:T(8,128)(2,1)S(1)} %fusion.22), channel_id=1, source_target_pairs={{0,2},{1,3},{2,4},{3,5},{4,0},{5,1},{6,8},{7,9},{8,10},{9,11},{10,... | collective-permute-start | bytes 442376 | tf_op jit(solution)/shard_map/ppermute | solution.py:46
  51.0 3.5 %collective-permute-start.3 = (bf16[3,192,128]{2,1,0:T(8,128)(2,1)S(1)}, bf16[3,192,128]{2,1,0:T(8,128)(2,1)S(1)}, u32[]{:S(2)}, u32[]{:S(2)}) collective-permute-start(bf16[3,192,128]{2,1,0:T(8,128)(2,1)S(1)} %fusion.22), channel_id=1, source_target_pairs={{0,4},{1,5},{2,0},{3,1},{4,2},{5,3},{6,10},{7,11},{8,6},{9,7},{10,... | collective-permute-start | bytes 442376 | tf_op jit(solution)/shard_map/ppermute | solution.py:47
  54.7 1.0 constant_dynamic-slice_fusion
  55.7 6.1 %collective-permute-done.2 = bf16[3,192,128]{2,1,0:T(8,128)(2,1)S(1)} collective-permute-done((bf16[3,192,128]{2,1,0:T(8,128)(2,1)S(1)}, bf16[3,192,128]{2,1,0:T(8,128)(2,1)S(1)}, u32[]{:S(2)}, u32[]{:S(2)}) %collective-permute-start.2) | collective-permute-done | bytes 147488 | tf_op jit(solution)/shard_map/ppermute | solution.py:46
  61.8 7.7 %collective-permute-done.3 = bf16[3,192,128]{2,1,0:T(8,128)(2,1)S(1)} collective-permute-done((bf16[3,192,128]{2,1,0:T(8,128)(2,1)S(1)}, bf16[3,192,128]{2,1,0:T(8,128)(2,1)S(1)}, u32[]{:S(2)}, u32[]{:S(2)}) %collective-permute-start.3) | collective-permute-done | bytes 147488 | tf_op jit(solution)/shard_map/ppermute | solution.py:47
  69.6 0.1 fusion.21
  69.7 0.2 copy.20
  69.9 2.2 %fusion.17 = (bf16[576,256]{1,0:T(8,128)(2,1)S(1)}, f32[576,256]{1,0:T(8,128)}, f32[576,256]{1,0:T(8,128)}) fusion(bf16[3,1,192,256]{3,2,1,0:T(8,128)(2,1)S(1)} %constant_dynamic-slice_fusion, bf16[576,128]{1,0:T(8,128)(2,1)S(1)} %fusion.21, bf16[128,256]{1,0:T(8,128)(2,1)} %param.10), kind=kOutput, calls=%fused_computation.11 | convolution fusion | flops 39223296 | bytes 1982464 | tf_op jit(solution)/shard_map/dot_general | solution.py:54
  72.1 0.2 fusion.18
  72.3 2.4 %collective-permute-start.9 = (f32[64,256]{1,0:T(8,128)S(1)}, f32[64,256]{1,0:T(8,128)S(1)}, u32[]{:S(2)}, u32[]{:S(2)}) collective-permute-start(f32[64,256]{1,0:T(8,128)S(1)} %dynamic-slice_bitcast_fusion), channel_id=1, source_target_pairs={{0,1},{1,0},{2,3},{3,2},{4,5},{5,4},{6,7},{7,6},{8,9},{9,8},{10,11... | collective-permute-start | bytes 196616 | tf_op jit(solution)/shard_map/ppermute | solution.py:28
  74.8 1.1 fusion.16
  75.8 1.9 %collective-permute-start.4 = (bf16[576,128]{1,0:T(8,128)(2,1)S(1)}, bf16[576,128]{1,0:T(8,128)(2,1)S(1)}, u32[]{:S(2)}, u32[]{:S(2)}) collective-permute-start(bf16[576,128]{1,0:T(8,128)(2,1)S(1)} %fusion.16), channel_id=1, source_target_pairs={{0,1},{1,0},{2,3},{3,2},{4,5},{5,4},{6,7},{7,6},{8,9},{9,8},{10,11... | collective-permute-start | bytes 442376 | tf_op jit(solution)/shard_map/ppermute | solution.py:28
  77.8 1.9 %collective-permute-start.10 = (f32[64,256]{1,0:T(8,128)S(1)}, f32[64,256]{1,0:T(8,128)S(1)}, u32[]{:S(2)}, u32[]{:S(2)}) collective-permute-start(f32[64,256]{1,0:T(8,128)S(1)} %bitcast_add_fusion.2), channel_id=1, source_target_pairs={{0,6},{6,0},{12,18},{18,12},{24,30},{30,24},{36,42},{42,36},{48,54... | collective-permute-start | bytes 196616 | tf_op jit(solution)/shard_map/ppermute | solution.py:76
  79.7 3.1 %collective-permute-done.10 = f32[64,256]{1,0:T(8,128)S(1)} collective-permute-done((f32[64,256]{1,0:T(8,128)S(1)}, f32[64,256]{1,0:T(8,128)S(1)}, u32[]{:S(2)}, u32[]{:S(2)}) %collective-permute-start.10) | collective-permute-done | bytes 65568 | tf_op jit(solution)/shard_map/ppermute | solution.py:76
  82.8 3.4 %collective-permute-start.11 = (f32[64,256]{1,0:T(8,128)S(1)}, f32[64,256]{1,0:T(8,128)S(1)}, u32[]{:S(2)}, u32[]{:S(2)}) collective-permute-start(f32[64,256]{1,0:T(8,128)S(1)} %add.123), channel_id=1, source_target_pairs={{0,12},{6,18},{12,0},{18,6},{24,36},{30,42},{36,24},{42,30},{48,60... | collective-permute-start | bytes 196616 | tf_op jit(solution)/shard_map/ppermute | solution.py:76
  86.4 3.0 %collective-permute-done.11 = f32[64,256]{1,0:T(8,128)S(1)} collective-permute-done((f32[64,256]{1,0:T(8,128)S(1)}, f32[64,256]{1,0:T(8,128)S(1)}, u32[]{:S(2)}, u32[]{:S(2)}) %collective-permute-start.11) | collective-permute-done | bytes 65568 | tf_op jit(solution)/shard_map/ppermute | solution.py:76
  89.4 6.2 %collective-permute-start.12 = (f32[64,256]{1,0:T(8,128)S(1)}, f32[64,256]{1,0:T(8,128)S(1)}, u32[]{:S(2)}, u32[]{:S(2)}) collective-permute-start(f32[64,256]{1,0:T(8,128)S(1)} %add.124), channel_id=1, source_target_pairs={{0,24},{6,30},{12,36},{18,42},{24,0},{30,6},{36,12},{42,18},{48,72... | collective-permute-start | bytes 196616 | tf_op jit(solution)/shard_map/ppermute | solution.py:76
  95.7 0.6 fusion.10
  96.3 1.0 copy.19
  97.3 1.0 collective-permute-done.12
  98.3 1.9 %collective-permute-start.13 = (f32[64,256]{1,0:T(8,128)S(1)}, f32[64,256]{1,0:T(8,128)S(1)}, u32[]{:S(2)}, u32[]{:S(2)}) collective-permute-start(f32[64,256]{1,0:T(8,128)S(1)} %add.125), channel_id=1, source_target_pairs={{0,48},{6,54},{12,60},{18,66},{24,72},{30,78},{36,84},{42,90},{48,... | collective-permute-start | bytes 196616 | tf_op jit(solution)/shard_map/ppermute | solution.py:76
  100.3 1.0 fusion.25
  101.3 10.8 %collective-permute-start.5 = (bf16[3,192,128]{2,1,0:T(8,128)(2,1)S(1)}, bf16[3,192,128]{2,1,0:T(8,128)(2,1)S(1)}, u32[]{:S(2)}, u32[]{:S(2)}) collective-permute-start(bf16[3,192,128]{2,1,0:T(8,128)(2,1)S(1)} %fusion.25), channel_id=1, source_target_pairs={{0,7},{1,762},{2,9},{3,764},{4,11},{5,766},{6,13},{7,0},{8,15},{9,... | collective-permute-start | bytes 442376 | tf_op jit(solution)/shard_map/ppermute | solution.py:25
  112.2 0.8 dynamic_slice.54
  113.0 2.2 %collective-permute-start.14 = (f32[64,256]{1,0:T(8,128)S(1)}, f32[64,256]{1,0:T(8,128)S(1)}, u32[]{:S(2)}, u32[]{:S(2)}) collective-permute-start(f32[64,256]{1,0:T(8,128)S(1)} %add.126), channel_id=1, source_target_pairs={{0,96},{6,102},{12,108},{18,114},{24,120},{30,126},{36,132},{42,13... | collective-permute-start | bytes 196616 | tf_op jit(solution)/shard_map/ppermute | solution.py:76
  115.1 1.7 %fusion.23 = bf16[192,256]{1,0:T(8,128)(2,1)} fusion(f32[576,256]{1,0:T(8,128)} %get-tuple-element.4, s32[]{:T(128)S(6)} %select_n.146, f32[576,256]{1,0:T(8,128)} %get-tuple-element.12), kind=kLoop, calls=%fused_computation.27 | loop fusion | flops 98304 | bytes 491524 | tf_op jit(solution)/shard_map/convert_element_type | solution.py:56
  116.8 2.1 %collective-permute-done.14 = f32[64,256]{1,0:T(8,128)S(1)} collective-permute-done((f32[64,256]{1,0:T(8,128)S(1)}, f32[64,256]{1,0:T(8,128)S(1)}, u32[]{:S(2)}, u32[]{:S(2)}) %collective-permute-start.14) | collective-permute-done | bytes 65568 | tf_op jit(solution)/shard_map/ppermute | solution.py:76
  118.9 1.9 %collective-permute-start.15 = (f32[64,256]{1,0:T(8,128)S(1)}, f32[64,256]{1,0:T(8,128)S(1)}, u32[]{:S(2)}, u32[]{:S(2)}) collective-permute-start(f32[64,256]{1,0:T(8,128)S(1)} %add.127), channel_id=1, source_target_pairs={{0,192},{6,198},{12,204},{18,210},{24,216},{30,222},{36,228},{42,2... | collective-permute-start | bytes 196616 | tf_op jit(solution)/shard_map/ppermute | solution.py:76
  120.8 1.0 fusion.20
  121.8 2.1 %collective-permute-done.15 = f32[64,256]{1,0:T(8,128)S(1)} collective-permute-done((f32[64,256]{1,0:T(8,128)S(1)}, f32[64,256]{1,0:T(8,128)S(1)}, u32[]{:S(2)}, u32[]{:S(2)}) %collective-permute-start.15) | collective-permute-done | bytes 65568 | tf_op jit(solution)/shard_map/ppermute | solution.py:76
  123.9 3.5 %collective-permute-start.16 = (f32[64,256]{1,0:T(8,128)S(1)}, f32[64,256]{1,0:T(8,128)S(1)}, u32[]{:S(2)}, u32[]{:S(2)}) collective-permute-start(f32[64,256]{1,0:T(8,128)S(1)} %add.128), channel_id=1, source_target_pairs={{0,384},{6,390},{12,396},{18,402},{24,408},{30,414},{36,420},{42,4... | collective-permute-start | bytes 196616 | tf_op jit(solution)/shard_map/ppermute | solution.py:76
  127.5 3.5 %collective-permute-start.8 = (bf16[192,128]{1,0:T(8,128)(2,1)S(1)}, bf16[192,128]{1,0:T(8,128)(2,1)S(1)}, u32[]{:S(2)}, u32[]{:S(2)}) collective-permute-start(bf16[192,128]{1,0:T(8,128)(2,1)S(1)} %get-tuple-element.8), channel_id=1, source_target_pairs={{0,4},{1,767},{2,756},{3,751},{4,746},{5,741},{6,10},{7,5},{8,762}... | collective-permute-start | bytes 147464 | tf_op jit(solution)/shard_map/ppermute | solution.py:25
  131.0 9.5 %collective-permute-start.7 = (bf16[192,128]{1,0:T(8,128)(2,1)S(1)}, bf16[192,128]{1,0:T(8,128)(2,1)S(1)}, u32[]{:S(2)}, u32[]{:S(2)}) collective-permute-start(bf16[192,128]{1,0:T(8,128)(2,1)S(1)} %get-tuple-element.9), channel_id=1, source_target_pairs={{0,2},{1,765},{2,760},{3,755},{4,744},{5,739},{6,8},{7,3},{8,766},... | collective-permute-start | bytes 147464 | tf_op jit(solution)/shard_map/ppermute | solution.py:25
  140.5 1.9 %collective-permute-start.6 = (bf16[192,128]{1,0:T(8,128)(2,1)S(1)}, bf16[192,128]{1,0:T(8,128)(2,1)S(1)}, u32[]{:S(2)}, u32[]{:S(2)}) collective-permute-start(bf16[192,128]{1,0:T(8,128)(2,1)S(1)} %get-tuple-element.7), channel_id=1, source_target_pairs={{0,0},{1,763},{2,758},{3,753},{4,748},{5,743},{6,6},{7,1},{8,764},... | collective-permute-start | bytes 147464 | tf_op jit(solution)/shard_map/ppermute | solution.py:25
  142.4 1.9 %collective-permute-start.17 = (f32[64,256]{1,0:T(8,128)S(1)}, f32[64,256]{1,0:T(8,128)S(1)}, u32[]{:S(2)}, u32[]{:S(2)}) collective-permute-start(f32[64,256]{1,0:T(8,128)S(1)} %add_multiply_fusion), channel_id=1, source_target_pairs={{0,1},{1,0},{2,3},{3,2},{4,5},{5,4},{6,7},{7,6},{8,9},{9,8},{10,11... | collective-permute-start | bytes 196616 | tf_op jit(solution)/shard_map/ppermute | solution.py:28
  144.4 1.4 collective-permute-done.7
  145.7 0.7 multiply_convert_fusion.1
  146.5 0.7 pad_maximum_fusion.1
  (33 shorter events, 0.5 us)
Async XLA Ops:
  0.6 19.7 %copy-start = (bf16[1,1152,1152]{2,1,0:T(8,128)(2,1)S(1)}, bf16[1,1152,1152]{2,1,0:T(8,128)(2,1)}, u32[]{:S(2)}) copy-start(bf16[1,1152,1152]{2,1,0:T(8,128)(2,1)} %param.8) | copy-start | bytes 7962628
  1.5 53.0 %copy-start.1 = (f32[1152]{0:T(1024)}, f32[1152]{0:T(1024)S(1)}, u32[]{:S(2)}) copy-start(f32[1152]{0:T(1024)S(1)} %convert_rsqrt_fusion) | copy-start | bytes 13828
  2.7 17.7 %collective-permute-start = (bf16[1152,128]{1,0:T(8,128)(2,1)S(1)}, bf16[1152,128]{1,0:T(8,128)(2,1)S(1)}, u32[]{:S(2)}, u32[]{:S(2)}) collective-permute-start(bf16[1152,128]{1,0:T(8,128)(2,1)S(1)} %multiply_convert_fusion), channel_id=1, source_target_pairs={{0,0},{1,7},{2,14},{3,21},{4,28},{5,35},{6,6},{7,13},{8,20},{9,27}... | collective-permute-start | bytes 884744 | tf_op jit(solution)/shard_map/ppermute | solution.py:25
  23.3 3.3 %collective-permute-start.1 = (bf16[3,192,128]{2,1,0:T(8,128)(2,1)S(1)}, bf16[3,192,128]{2,1,0:T(8,128)(2,1)S(1)}, u32[]{:S(2)}, u32[]{:S(2)}) collective-permute-start(bf16[3,192,128]{2,1,0:T(8,128)(2,1)S(1)} %fusion.24), channel_id=1, source_target_pairs={{0,1},{1,0},{2,3},{3,2},{4,5},{5,4},{6,7},{7,6},{8,9},{9,8},{10,11... | collective-permute-start | bytes 442376 | tf_op jit(solution)/shard_map/ppermute | solution.py:28
  27.6 34.2 %collective-permute-start.2 = (bf16[3,192,128]{2,1,0:T(8,128)(2,1)S(1)}, bf16[3,192,128]{2,1,0:T(8,128)(2,1)S(1)}, u32[]{:S(2)}, u32[]{:S(2)}) collective-permute-start(bf16[3,192,128]{2,1,0:T(8,128)(2,1)S(1)} %fusion.22), channel_id=1, source_target_pairs={{0,2},{1,3},{2,4},{3,5},{4,0},{5,1},{6,8},{7,9},{8,10},{9,11},{10,... | collective-permute-start | bytes 442376 | tf_op jit(solution)/shard_map/ppermute | solution.py:46
  51.0 18.5 %collective-permute-start.3 = (bf16[3,192,128]{2,1,0:T(8,128)(2,1)S(1)}, bf16[3,192,128]{2,1,0:T(8,128)(2,1)S(1)}, u32[]{:S(2)}, u32[]{:S(2)}) collective-permute-start(bf16[3,192,128]{2,1,0:T(8,128)(2,1)S(1)} %fusion.22), channel_id=1, source_target_pairs={{0,4},{1,5},{2,0},{3,1},{4,2},{5,3},{6,10},{7,11},{8,6},{9,7},{10,... | collective-permute-start | bytes 442376 | tf_op jit(solution)/shard_map/ppermute | solution.py:47
  54.7 15.1 %copy-start.2 = (f32[576]{0:T(1024)}, f32[576]{0:T(1024)S(1)}, u32[]{:S(2)}) copy-start(f32[576]{0:T(1024)S(1)} %mul.77) | copy-start | bytes 6916
  69.9 4.8 %copy-start.3 = (f32[576]{0:T(1024)S(1)}, f32[576]{0:T(1024)}, u32[]{:S(2)}) copy-start(f32[576]{0:T(1024)} %copy-done.2) | copy-start | bytes 6916
  72.3 5.4 %collective-permute-start.9 = (f32[64,256]{1,0:T(8,128)S(1)}, f32[64,256]{1,0:T(8,128)S(1)}, u32[]{:S(2)}, u32[]{:S(2)}) collective-permute-start(f32[64,256]{1,0:T(8,128)S(1)} %dynamic-slice_bitcast_fusion), channel_id=1, source_target_pairs={{0,1},{1,0},{2,3},{3,2},{4,5},{5,4},{6,7},{7,6},{8,9},{9,8},{10,11... | collective-permute-start | bytes 196616 | tf_op jit(solution)/shard_map/ppermute | solution.py:28
  75.8 10.4 %collective-permute-start.4 = (bf16[576,128]{1,0:T(8,128)(2,1)S(1)}, bf16[576,128]{1,0:T(8,128)(2,1)S(1)}, u32[]{:S(2)}, u32[]{:S(2)}) collective-permute-start(bf16[576,128]{1,0:T(8,128)(2,1)S(1)} %fusion.16), channel_id=1, source_target_pairs={{0,1},{1,0},{2,3},{3,2},{4,5},{5,4},{6,7},{7,6},{8,9},{9,8},{10,11... | collective-permute-start | bytes 442376 | tf_op jit(solution)/shard_map/ppermute | solution.py:28
  77.8 5.0 %collective-permute-start.10 = (f32[64,256]{1,0:T(8,128)S(1)}, f32[64,256]{1,0:T(8,128)S(1)}, u32[]{:S(2)}, u32[]{:S(2)}) collective-permute-start(f32[64,256]{1,0:T(8,128)S(1)} %bitcast_add_fusion.2), channel_id=1, source_target_pairs={{0,6},{6,0},{12,18},{18,12},{24,30},{30,24},{36,42},{42,36},{48,54... | collective-permute-start | bytes 196616 | tf_op jit(solution)/shard_map/ppermute | solution.py:76
  82.8 6.6 %collective-permute-start.11 = (f32[64,256]{1,0:T(8,128)S(1)}, f32[64,256]{1,0:T(8,128)S(1)}, u32[]{:S(2)}, u32[]{:S(2)}) collective-permute-start(f32[64,256]{1,0:T(8,128)S(1)} %add.123), channel_id=1, source_target_pairs={{0,12},{6,18},{12,0},{18,6},{24,36},{30,42},{36,24},{42,30},{48,60... | collective-permute-start | bytes 196616 | tf_op jit(solution)/shard_map/ppermute | solution.py:76
  89.4 8.9 %collective-permute-start.12 = (f32[64,256]{1,0:T(8,128)S(1)}, f32[64,256]{1,0:T(8,128)S(1)}, u32[]{:S(2)}, u32[]{:S(2)}) collective-permute-start(f32[64,256]{1,0:T(8,128)S(1)} %add.124), channel_id=1, source_target_pairs={{0,24},{6,30},{12,36},{18,42},{24,0},{30,6},{36,12},{42,18},{48,72... | collective-permute-start | bytes 196616 | tf_op jit(solution)/shard_map/ppermute | solution.py:76
  98.3 14.6 %collective-permute-start.13 = (f32[64,256]{1,0:T(8,128)S(1)}, f32[64,256]{1,0:T(8,128)S(1)}, u32[]{:S(2)}, u32[]{:S(2)}) collective-permute-start(f32[64,256]{1,0:T(8,128)S(1)} %add.125), channel_id=1, source_target_pairs={{0,48},{6,54},{12,60},{18,66},{24,72},{30,78},{36,84},{42,90},{48,... | collective-permute-start | bytes 196616 | tf_op jit(solution)/shard_map/ppermute | solution.py:76
  101.3 19.6 %collective-permute-start.5 = (bf16[3,192,128]{2,1,0:T(8,128)(2,1)S(1)}, bf16[3,192,128]{2,1,0:T(8,128)(2,1)S(1)}, u32[]{:S(2)}, u32[]{:S(2)}) collective-permute-start(bf16[3,192,128]{2,1,0:T(8,128)(2,1)S(1)} %fusion.25), channel_id=1, source_target_pairs={{0,7},{1,762},{2,9},{3,764},{4,11},{5,766},{6,13},{7,0},{8,15},{9,... | collective-permute-start | bytes 442376 | tf_op jit(solution)/shard_map/ppermute | solution.py:25
  113.0 5.9 %collective-permute-start.14 = (f32[64,256]{1,0:T(8,128)S(1)}, f32[64,256]{1,0:T(8,128)S(1)}, u32[]{:S(2)}, u32[]{:S(2)}) collective-permute-start(f32[64,256]{1,0:T(8,128)S(1)} %add.126), channel_id=1, source_target_pairs={{0,96},{6,102},{12,108},{18,114},{24,120},{30,126},{36,132},{42,13... | collective-permute-start | bytes 196616 | tf_op jit(solution)/shard_map/ppermute | solution.py:76
  118.9 5.0 %collective-permute-start.15 = (f32[64,256]{1,0:T(8,128)S(1)}, f32[64,256]{1,0:T(8,128)S(1)}, u32[]{:S(2)}, u32[]{:S(2)}) collective-permute-start(f32[64,256]{1,0:T(8,128)S(1)} %add.127), channel_id=1, source_target_pairs={{0,192},{6,198},{12,204},{18,210},{24,216},{30,222},{36,228},{42,2... | collective-permute-start | bytes 196616 | tf_op jit(solution)/shard_map/ppermute | solution.py:76
  123.9 18.5 %collective-permute-start.16 = (f32[64,256]{1,0:T(8,128)S(1)}, f32[64,256]{1,0:T(8,128)S(1)}, u32[]{:S(2)}, u32[]{:S(2)}) collective-permute-start(f32[64,256]{1,0:T(8,128)S(1)} %add.128), channel_id=1, source_target_pairs={{0,384},{6,390},{12,396},{18,402},{24,408},{30,414},{36,420},{42,4... | collective-permute-start | bytes 196616 | tf_op jit(solution)/shard_map/ppermute | solution.py:76
  127.5 16.9 %collective-permute-start.8 = (bf16[192,128]{1,0:T(8,128)(2,1)S(1)}, bf16[192,128]{1,0:T(8,128)(2,1)S(1)}, u32[]{:S(2)}, u32[]{:S(2)}) collective-permute-start(bf16[192,128]{1,0:T(8,128)(2,1)S(1)} %get-tuple-element.8), channel_id=1, source_target_pairs={{0,4},{1,767},{2,756},{3,751},{4,746},{5,741},{6,10},{7,5},{8,762}... | collective-permute-start | bytes 147464 | tf_op jit(solution)/shard_map/ppermute | solution.py:25
  131.0 14.8 %collective-permute-start.7 = (bf16[192,128]{1,0:T(8,128)(2,1)S(1)}, bf16[192,128]{1,0:T(8,128)(2,1)S(1)}, u32[]{:S(2)}, u32[]{:S(2)}) collective-permute-start(bf16[192,128]{1,0:T(8,128)(2,1)S(1)} %get-tuple-element.9), channel_id=1, source_target_pairs={{0,2},{1,765},{2,760},{3,755},{4,744},{5,739},{6,8},{7,3},{8,766},... | collective-permute-start | bytes 147464 | tf_op jit(solution)/shard_map/ppermute | solution.py:25
  140.5 5.3 %collective-permute-start.6 = (bf16[192,128]{1,0:T(8,128)(2,1)S(1)}, bf16[192,128]{1,0:T(8,128)(2,1)S(1)}, u32[]{:S(2)}, u32[]{:S(2)}) collective-permute-start(bf16[192,128]{1,0:T(8,128)(2,1)S(1)} %get-tuple-element.7), channel_id=1, source_target_pairs={{0,0},{1,763},{2,758},{3,753},{4,748},{5,743},{6,6},{7,1},{8,764},... | collective-permute-start | bytes 147464 | tf_op jit(solution)/shard_map/ppermute | solution.py:25
  142.4 4.0 %collective-permute-start.17 = (f32[64,256]{1,0:T(8,128)S(1)}, f32[64,256]{1,0:T(8,128)S(1)}, u32[]{:S(2)}, u32[]{:S(2)}) collective-permute-start(f32[64,256]{1,0:T(8,128)S(1)} %add_multiply_fusion), channel_id=1, source_target_pairs={{0,1},{1,0},{2,3},{3,2},{4,5},{5,4},{6,7},{7,6},{8,9},{9,8},{10,11... | collective-permute-start | bytes 196616 | tf_op jit(solution)/shard_map/ppermute | solution.py:28

commit v2 on v1

v2 whole, which is shorter than its diff:
```python
import math

import jax
import jax.numpy as jnp
from jax import lax
from jax.sharding import PartitionSpec as P

BF = jnp.bfloat16
F32 = jnp.float32


def local(features, degrees, tiles, pattern, weight, cotangent):
    teams = lax.axis_size("team")
    reps = lax.axis_size("rep")
    zs = reps // 2
    rep = lax.axis_index("rep")
    z, core = rep // 2, rep % 2
    rows, feat = features.shape
    hid = weight.shape[1]
    own = rows // reps
    half = zs * own

    def across(value, move):
        route = [(i * reps + s, (move(i, s)[0] % teams) * reps + move(i, s)[1]) for i in range(teams) for s in range(reps)]
        return lax.ppermute(value, ("team", "rep"), route)

    def swap_core(value):
        return lax.ppermute(value, "rep", [(s, s ^ 1) for s in range(reps)])

    def pair_move(i, s):
        return (i + 1 if s % 2 == 0 else i - 1, s ^ 1)

    def pick(array, which):
        return lax.dynamic_index_in_dim(array, which, 1, keepdims=False)

    inv_root = 1.0 / jnp.sqrt(degrees.astype(F32))
    inv_half = pick(inv_root.reshape(zs, 2, own), core).reshape(half)
    inv_own = lax.dynamic_slice_in_dim(inv_root, rep * own, own, 0)
    source = (features.astype(F32) * inv_root[:, None]).astype(BF)
    tile_on = pattern[0, 0].astype(F32)
    tile = tiles[0]

    mid = rows // 2
    sent = lax.dynamic_slice_in_dim(source, core * mid, mid, 0)
    held = across(sent, lambda i, s: (i + s, s))
    other = across(held, pair_move)
    block = jnp.concatenate([jnp.where(core == 0, held, other), jnp.where(core == 0, other, held)], axis=0)
    partial = jnp.dot(tile, block, preferred_element_type=F32) * tile_on
    parts = partial.reshape(zs, 2, own, feat)

    chip = pick(parts, core) + swap_core(pick(parts, 1 - core).astype(BF)).astype(F32)
    sent = chip.astype(BF)
    from1 = lax.ppermute(sent, "rep", [(s, (s + 2) % reps) for s in range(reps)])
    from2 = lax.ppermute(sent, "rep", [(s, (s + 4) % reps) for s in range(reps)])
    first = jnp.where(z == 0, sent, jnp.where(z == 1, from1, from2)).astype(F32)
    second = jnp.where(z == 1, sent, jnp.where(z == 2, from1, from2)).astype(F32)
    third = jnp.where(z == 2, sent, jnp.where(z == 0, from1, from2)).astype(F32)
    totals = (first + second + third).reshape(half, feat)

    agg_half = (totals * inv_half[:, None]).astype(BF)
    agg_other = swap_core(agg_half)
    mine, other = agg_half.reshape(zs, 1, own, feat), agg_other.reshape(zs, 1, own, feat)
    even, odd = jnp.where(core == 0, mine, other), jnp.where(core == 0, other, mine)
    aggregated = jnp.concatenate([even, odd], axis=1).reshape(rows, feat)

    pre_act = jnp.dot(aggregated, weight, preferred_element_type=F32)
    sig = jax.nn.sigmoid(pre_act)
    hidden = lax.dynamic_slice_in_dim((pre_act * sig).astype(BF), rep * own, own, 0)
    slope = (cotangent.astype(F32) * (sig * (1.0 + pre_act * (1.0 - sig)))).astype(BF)
    message = (
        lax.dot_general(slope, weight, (((1,), (1,)), ((), ())), preferred_element_type=F32) * inv_root[:, None]
    ).astype(BF)
    grad_part = lax.dot_general(aggregated, slope, (((0,), (0,)), ((), ())), preferred_element_type=F32)

    grad = lax.dynamic_slice_in_dim(grad_part, core * (feat // 2), feat // 2, 0)

    def pair_sum(value, bit):
        return value + lax.ppermute(value, "team", [(i, i ^ bit) for i in range(teams)])

    bits = [1 << b for b in range((teams - 1).bit_length())]
    grad = pair_sum(grad, bits[0])
    back = lax.dot_general(tile, message, (((0,), (0,)), ((), ())), preferred_element_type=F32) * tile_on
    backs = back.reshape(zs, 2, own, feat)
    keep, give = pick(backs, core), pick(backs, 1 - core).astype(BF)
    grad, keep, give = lax.optimization_barrier((grad, keep, give))
    taken = across(give, pair_move)
    grad = pair_sum(grad, bits[1])
    sent = (keep + taken.astype(F32)).astype(BF)
    grad, sent = lax.optimization_barrier((grad, sent))
    got = []
    for k in range(zs):
        chunk = lax.dynamic_index_in_dim(sent, (z + k) % zs, 0, keepdims=False)
        got.append(across(chunk, lambda i, s: (i - s, 2 * ((s // 2 + k) % zs) + s % 2)))
    for bit in bits[2:4]:
        grad = pair_sum(grad, bit)
    grad, got = lax.optimization_barrier((grad, got))
    summed = sum(g.astype(F32) for g in got)
    grad_features = (summed * inv_own[:, None]).astype(BF)
    for bit in bits[4:]:
        grad = pair_sum(grad, bit)
    grad = grad * (1.0 / math.sqrt(rows * teams))
    grad_other = swap_core(grad)
    grad_weight = jnp.concatenate(
        [jnp.where(core == 0, grad, grad_other), jnp.where(core == 0, grad_other, grad)], axis=0
    )
    return (hidden, grad_features, grad_weight)


def solution(mesh):
    in_specs = (
        P("team", None),
        P("team"),
        P("rep", "team", None),
        P("rep", "team"),
        P(),
        P("team", None),
    )
    out_specs = (P(("team", "rep"), None), P(("team", "rep"), None), P())
    return jax.shard_map(local, mesh=mesh, in_specs=in_specs, out_specs=out_specs, check_vma=False)
```

time: 148 us -> 161 us (1.088)
  waiting for transfers between devices: 40.7 us -> 71 us
  starting transfers between devices: 85.9 us -> 68.9 us
    ppermute x5 -> x6, waiting for transfers between devices: 14.3 us -> 32.6 us  [across(): return lax.ppermute(value, ('team', 'rep'), route)]
    ppermute x7, waiting for transfers between devices: 11.2 us -> 23.6 us  [pair_sum(): lax.ppermute(value, 'team', [(i, i ^ bit) for i in range(teams)])]
    ppermute x7, starting transfers between devices: 21.1 us -> 13.4 us  [pair_sum(): lax.ppermute(value, 'team', [(i, i ^ bit) for i in range(teams)])]
    ppermute x1, starting transfers between devices: 23.3 us -> 15.9 us  [local(): lax.ppermute(sent, 'rep', [(s, (s + 2) % reps) for s in range(reps)])]
    ppermute x1, waiting for transfers between devices: 7.73 us -> 3.21 us  [local(): lax.ppermute(sent, 'rep', [(s, (s + 4) % reps) for s in range(reps)])]
    ppermute x1, waiting for transfers between devices: 6.11 us -> 9.26 us  [local(): lax.ppermute(sent, 'rep', [(s, (s + 2) % reps) for s in range(reps)])]
    ppermute x4 -> x3, starting transfers between devices: 8.17 us -> 7.77 us  [swap_core(): return lax.ppermute(value, 'rep', [(s, s ^ 1) for s in range(reps)])]
    ppermute x5 -> x6, starting transfers between devices: 29.8 us -> 29.9 us  [across(): return lax.ppermute(value, ('team', 'rep'), route)]
  transfers between devices with their start and end apart: 18 -> 18, of which waited for: 10 -> 14; matrix products, arithmetic and copies ran while one was open for 6% -> 4% of each run, Pallas kernels for 0% -> 0%
where the time goes in v2:
time: 161 us; the launch traced here: 160 us
  waiting for transfers between devices  71 us (44%)
  starting transfers between devices  68.9 us (43%)
  other arithmetic  6.52 us (4%)
  local copies, waits for them, and re-layouts  6.34 us (4%)
  matrix products  5.22 us (3%)
  between operations  1.8 us (1%)
    ppermute x6, waiting for transfers between devices, across(): return lax.ppermute(value, ('team', 'rep'), route)  32.6 us
    ppermute x6, starting transfers between devices, across(): return lax.ppermute(value, ('team', 'rep'), route)  29.9 us
    ppermute x7, waiting for transfers between devices, pair_sum(): lax.ppermute(value, 'team', [(i, i ^ bit) for i in range(teams)])  23.6 us
    ppermute x1, starting transfers between devices, local(): lax.ppermute(sent, 'rep', [(s, (s + 2) % reps) for s in range(reps)])  15.9 us
    ppermute x7, starting transfers between devices, pair_sum(): lax.ppermute(value, 'team', [(i, i ^ bit) for i in range(teams)])  13.4 us
    ppermute x1, waiting for transfers between devices, local(): lax.ppermute(sent, 'rep', [(s, (s + 2) % reps) for s in range(reps)])  9.26 us
    ppermute x3, starting transfers between devices, swap_core(): return lax.ppermute(value, 'rep', [(s, s ^ 1) for s in range(reps)])  7.77 us
  transfers between devices with their start and end apart: 18, of which 14 were waited for; matrix products, arithmetic and copies ran while one was open for 4% of the time, Pallas kernels for 0%

profile of v2, /device:TPU:1, one launch (start us, length us, event | category | flops | bytes accessed | tf_op | source)
XLA Modules:
  0.0 159.8 jit_solution(8635442600389122442)
XLA Ops:
  0.7 0.9 convert_rsqrt_fusion
  1.6 1.1 multiply_convert_fusion.2
  2.7 4.0 %collective-permute-start = (bf16[576,128]{1,0:T(8,128)(2,1)S(1)}, bf16[576,128]{1,0:T(8,128)(2,1)S(1)}, u32[]{:S(2)}, u32[]{:S(2)}) collective-permute-start(bf16[576,128]{1,0:T(8,128)(2,1)S(1)} %multiply_convert_fusion.2), channel_id=1, source_target_pairs={{0,0},{1,7},{2,14},{3,21},{4,28},{5,35},{6,6},{7,13},{8,20},{9,27}... | collective-permute-start | bytes 442376 | tf_op jit(solution)/shard_map/ppermute | solution.py:25
  6.7 12.0 %collective-permute-done = bf16[576,128]{1,0:T(8,128)(2,1)S(1)} collective-permute-done((bf16[576,128]{1,0:T(8,128)(2,1)S(1)}, bf16[576,128]{1,0:T(8,128)(2,1)S(1)}, u32[]{:S(2)}, u32[]{:S(2)}) %collective-permute-start) | collective-permute-done | bytes 147488 | tf_op jit(solution)/shard_map/ppermute | solution.py:25
  18.7 1.9 %collective-permute-start.1 = (bf16[576,128]{1,0:T(8,128)(2,1)S(1)}, bf16[576,128]{1,0:T(8,128)(2,1)S(1)}, u32[]{:S(2)}, u32[]{:S(2)}) collective-permute-start(bf16[576,128]{1,0:T(8,128)(2,1)S(1)} %collective-permute-done), channel_id=1, source_target_pairs={{0,7},{1,762},{2,9},{3,764},{4,11},{5,766},{6,13},{7,0},{8,15},{9,... | collective-permute-start | bytes 442376 | tf_op jit(solution)/shard_map/ppermute | solution.py:25
  21.3 9.9 %collective-permute-done.1 = bf16[576,128]{1,0:T(8,128)(2,1)S(1)} collective-permute-done((bf16[576,128]{1,0:T(8,128)(2,1)S(1)}, bf16[576,128]{1,0:T(8,128)(2,1)S(1)}, u32[]{:S(2)}, u32[]{:S(2)}) %collective-permute-start.1) | collective-permute-done | bytes 147488 | tf_op jit(solution)/shard_map/ppermute | solution.py:25
  31.2 1.0 fusion.13
  32.2 1.1 copy.12
  33.3 1.0 fusion.24
  34.3 1.9 %collective-permute-start.2 = (bf16[3,192,128]{2,1,0:T(8,128)(2,1)S(1)}, bf16[3,192,128]{2,1,0:T(8,128)(2,1)S(1)}, u32[]{:S(2)}, u32[]{:S(2)}) collective-permute-start(bf16[3,192,128]{2,1,0:T(8,128)(2,1)S(1)} %fusion.24), channel_id=1, source_target_pairs={{0,1},{1,0},{2,3},{3,2},{4,5},{5,4},{6,7},{7,6},{8,9},{9,8},{10,11... | collective-permute-start | bytes 442376 | tf_op jit(solution)/shard_map/ppermute | solution.py:28
  36.2 1.3 collective-permute-done.2
  37.5 1.0 fusion.21
  38.5 15.9 %collective-permute-start.3 = (bf16[3,192,128]{2,1,0:T(8,128)(2,1)S(1)}, bf16[3,192,128]{2,1,0:T(8,128)(2,1)S(1)}, u32[]{:S(2)}, u32[]{:S(2)}) collective-permute-start(bf16[3,192,128]{2,1,0:T(8,128)(2,1)S(1)} %fusion.21), channel_id=1, source_target_pairs={{0,2},{1,3},{2,4},{3,5},{4,0},{5,1},{6,8},{7,9},{8,10},{9,11},{10,... | collective-permute-start | bytes 442376 | tf_op jit(solution)/shard_map/ppermute | solution.py:53
  54.4 1.9 %collective-permute-start.4 = (bf16[3,192,128]{2,1,0:T(8,128)(2,1)S(1)}, bf16[3,192,128]{2,1,0:T(8,128)(2,1)S(1)}, u32[]{:S(2)}, u32[]{:S(2)}) collective-permute-start(bf16[3,192,128]{2,1,0:T(8,128)(2,1)S(1)} %fusion.21), channel_id=1, source_target_pairs={{0,4},{1,5},{2,0},{3,1},{4,2},{5,3},{6,10},{7,11},{8,6},{9,7},{10,... | collective-permute-start | bytes 442376 | tf_op jit(solution)/shard_map/ppermute | solution.py:54
  56.6 9.3 %collective-permute-done.3 = bf16[3,192,128]{2,1,0:T(8,128)(2,1)S(1)} collective-permute-done((bf16[3,192,128]{2,1,0:T(8,128)(2,1)S(1)}, bf16[3,192,128]{2,1,0:T(8,128)(2,1)S(1)}, u32[]{:S(2)}, u32[]{:S(2)}) %collective-permute-start.3) | collective-permute-done | bytes 147488 | tf_op jit(solution)/shard_map/ppermute | solution.py:53
  65.8 3.2 %collective-permute-done.4 = bf16[3,192,128]{2,1,0:T(8,128)(2,1)S(1)} collective-permute-done((bf16[3,192,128]{2,1,0:T(8,128)(2,1)S(1)}, bf16[3,192,128]{2,1,0:T(8,128)(2,1)S(1)}, u32[]{:S(2)}, u32[]{:S(2)}) %collective-permute-start.4) | collective-permute-done | bytes 147488 | tf_op jit(solution)/shard_map/ppermute | solution.py:54
  69.3 2.4 %collective-permute-start.5 = (bf16[576,128]{1,0:T(8,128)(2,1)S(1)}, bf16[576,128]{1,0:T(8,128)(2,1)S(1)}, u32[]{:S(2)}, u32[]{:S(2)}) collective-permute-start(bf16[576,128]{1,0:T(8,128)(2,1)S(1)} %fusion.20), channel_id=1, source_target_pairs={{0,1},{1,0},{2,3},{3,2},{4,5},{5,4},{6,7},{7,6},{8,9},{9,8},{10,11... | collective-permute-start | bytes 442376 | tf_op jit(solution)/shard_map/ppermute | solution.py:28
  71.7 1.0 collective-permute-done.5
  72.9 1.9 %multiply_convert_fusion = (bf16[1152,256]{1,0:T(8,128)(2,1)S(1)}, f32[1152,256]{1,0:T(8,128)}, f32[1152,256]{1,0:T(8,128)}) fusion(bf16[1152,256]{1,0:T(8,128)(2,1)S(1)} %copy-done.3, bf16[1152,128]{1,0:T(8,128)(2,1)S(1)} %bitcast.59, bf16[128,256]{1,0:T(8,128)(2,1)S(1)} %copy-done.2), kind=kOutput, calls=%fused_computation.10 | convolution fusion | flops 78446592 | bytes 3899392 | tf_op jit(solution)/shard_map/dot_general | solution.py:66
  74.8 0.8 copy-done.1
  75.6 0.3 fusion.28
  75.9 2.1 %fusion.10 = f32[1152,128]{0,1:T(8,128)S(1)} fusion(bf16[1,1152,1152]{2,1,0:T(8,128)(2,1)S(1)} %copy-done, bf16[1152,256]{1,0:T(8,128)(2,1)} %copy-done.1, bf16[128,256]{1,0:T(8,128)(2,1)S(1)} %copy-done.2, f32[]{:T(128)} %bitcast.1, f32[1152]{0:T(1024)S(1)} %convert_rsqrt_fusion), kind=kOutput, calls=%fused_computation.7 | convolution fusion | flops 415678464 | bytes 3904004 | tf_op jit(solution)/shard_map/dot_general | solution.py:82
  78.0 1.9 %collective-permute-start.6 = (f32[64,256]{1,0:T(8,128)S(1)}, f32[64,256]{1,0:T(8,128)S(1)}, u32[]{:S(2)}, u32[]{:S(2)}) collective-permute-start(f32[64,256]{1,0:T(8,128)S(1)} %constant_dynamic-slice_fusion), channel_id=1, source_target_pairs={{0,6},{6,0},{12,18},{18,12},{24,30},{30,24},{36,42},{42,36},{48,54... | collective-permute-start | bytes 196616 | tf_op jit(solution)/shard_map/ppermute | solution.py:78
  80.0 1.1 copy.14
  81.0 1.0 dynamic-slice_bitcast_fusion
  82.0 1.0 fusion.25
  83.1 12.4 %collective-permute-start.8 = (bf16[3,192,128]{2,1,0:T(8,128)(2,1)S(1)}, bf16[3,192,128]{2,1,0:T(8,128)(2,1)S(1)}, u32[]{:S(2)}, u32[]{:S(2)}) collective-permute-start(bf16[3,192,128]{2,1,0:T(8,128)(2,1)S(1)} %fusion.25), channel_id=1, source_target_pairs={{0,7},{1,762},{2,9},{3,764},{4,11},{5,766},{6,13},{7,0},{8,15},{9,... | collective-permute-start | bytes 442376 | tf_op jit(solution)/shard_map/ppermute | solution.py:25
  95.4 1.9 %collective-permute-start.7 = (f32[64,256]{1,0:T(8,128)S(1)}, f32[64,256]{1,0:T(8,128)S(1)}, u32[]{:S(2)}, u32[]{:S(2)}) collective-permute-start(f32[64,256]{1,0:T(8,128)S(1)} %fusion.35), channel_id=1, source_target_pairs={{0,12},{6,18},{12,0},{18,6},{24,36},{30,42},{36,24},{42,30},{48,60... | collective-permute-start | bytes 196616 | tf_op jit(solution)/shard_map/ppermute | solution.py:78
  97.4 5.7 %collective-permute-done.7 = f32[64,256]{1,0:T(8,128)S(1)} collective-permute-done((f32[64,256]{1,0:T(8,128)S(1)}, f32[64,256]{1,0:T(8,128)S(1)}, u32[]{:S(2)}, u32[]{:S(2)}) %collective-permute-start.7) | collective-permute-done | bytes 65568 | tf_op jit(solution)/shard_map/ppermute | solution.py:78
  103.2 1.9 %collective-permute-start.9 = (f32[64,256]{1,0:T(8,128)S(1)}, f32[64,256]{1,0:T(8,128)S(1)}, u32[]{:S(2)}, u32[]{:S(2)}) collective-permute-start(f32[64,256]{1,0:T(8,128)S(1)} %add.109), channel_id=1, source_target_pairs={{0,24},{6,30},{12,36},{18,42},{24,0},{30,6},{36,12},{42,18},{48,72... | collective-permute-start | bytes 196616 | tf_op jit(solution)/shard_map/ppermute | solution.py:78
  105.1 6.9 %collective-permute-done.9 = f32[64,256]{1,0:T(8,128)S(1)} collective-permute-done((f32[64,256]{1,0:T(8,128)S(1)}, f32[64,256]{1,0:T(8,128)S(1)}, u32[]{:S(2)}, u32[]{:S(2)}) %collective-permute-start.9) | collective-permute-done | bytes 65568 | tf_op jit(solution)/shard_map/ppermute | solution.py:78
  112.1 1.9 %collective-permute-start.10 = (f32[64,256]{1,0:T(8,128)S(1)}, f32[64,256]{1,0:T(8,128)S(1)}, u32[]{:S(2)}, u32[]{:S(2)}) collective-permute-start(f32[64,256]{1,0:T(8,128)S(1)} %add.111), channel_id=1, source_target_pairs={{0,48},{6,54},{12,60},{18,66},{24,72},{30,78},{36,84},{42,90},{48,... | collective-permute-start | bytes 196616 | tf_op jit(solution)/shard_map/ppermute | solution.py:78
  114.0 2.4 %collective-permute-start.11 = (bf16[192,128]{1,0:T(8,128)(2,1)S(1)}, bf16[192,128]{1,0:T(8,128)(2,1)S(1)}, u32[]{:S(2)}, u32[]{:S(2)}) collective-permute-start(bf16[192,128]{1,0:T(8,128)(2,1)S(1)} %get-tuple-element.31), channel_id=1, source_target_pairs={{0,0},{1,763},{2,758},{3,753},{4,748},{5,743},{6,6},{7,1},{8,764},... | collective-permute-start | bytes 147464 | tf_op jit(solution)/shard_map/ppermute | solution.py:25
  116.5 7.3 %collective-permute-start.12 = (bf16[192,128]{1,0:T(8,128)(2,1)S(1)}, bf16[192,128]{1,0:T(8,128)(2,1)S(1)}, u32[]{:S(2)}, u32[]{:S(2)}) collective-permute-start(bf16[192,128]{1,0:T(8,128)(2,1)S(1)} %get-tuple-element.30), channel_id=1, source_target_pairs={{0,2},{1,765},{2,760},{3,755},{4,744},{5,739},{6,8},{7,3},{8,766},... | collective-permute-start | bytes 147464 | tf_op jit(solution)/shard_map/ppermute | solution.py:25
  123.7 1.9 %collective-permute-start.13 = (bf16[192,128]{1,0:T(8,128)(2,1)S(1)}, bf16[192,128]{1,0:T(8,128)(2,1)S(1)}, u32[]{:S(2)}, u32[]{:S(2)}) collective-permute-start(bf16[192,128]{1,0:T(8,128)(2,1)S(1)} %get-tuple-element.29), channel_id=1, source_target_pairs={{0,4},{1,767},{2,756},{3,751},{4,746},{5,741},{6,10},{7,5},{8,762}... | collective-permute-start | bytes 147464 | tf_op jit(solution)/shard_map/ppermute | solution.py:25
  125.7 4.3 %collective-permute-done.12 = bf16[192,128]{1,0:T(8,128)(2,1)S(1)} collective-permute-done((bf16[192,128]{1,0:T(8,128)(2,1)S(1)}, bf16[192,128]{1,0:T(8,128)(2,1)S(1)}, u32[]{:S(2)}, u32[]{:S(2)}) %collective-permute-start.12) | collective-permute-done | bytes 49184 | tf_op jit(solution)/shard_map/ppermute | solution.py:25
  129.9 6.4 %collective-permute-done.13 = bf16[192,128]{1,0:T(8,128)(2,1)S(1)} collective-permute-done((bf16[192,128]{1,0:T(8,128)(2,1)S(1)}, bf16[192,128]{1,0:T(8,128)(2,1)S(1)}, u32[]{:S(2)}, u32[]{:S(2)}) %collective-permute-start.13) | collective-permute-done | bytes 49184 | tf_op jit(solution)/shard_map/ppermute | solution.py:25
  136.3 1.9 %collective-permute-start.14 = (f32[64,256]{1,0:T(8,128)S(1)}, f32[64,256]{1,0:T(8,128)S(1)}, u32[]{:S(2)}, u32[]{:S(2)}) collective-permute-start(f32[64,256]{1,0:T(8,128)S(1)} %add.112), channel_id=1, source_target_pairs={{0,96},{6,102},{12,108},{18,114},{24,120},{30,126},{36,132},{42,13... | collective-permute-start | bytes 196616 | tf_op jit(solution)/shard_map/ppermute | solution.py:78
  138.2 4.0 %collective-permute-done.14 = f32[64,256]{1,0:T(8,128)S(1)} collective-permute-done((f32[64,256]{1,0:T(8,128)S(1)}, f32[64,256]{1,0:T(8,128)S(1)}, u32[]{:S(2)}, u32[]{:S(2)}) %collective-permute-start.14) | collective-permute-done | bytes 65568 | tf_op jit(solution)/shard_map/ppermute | solution.py:78
  142.2 1.9 %collective-permute-start.15 = (f32[64,256]{1,0:T(8,128)S(1)}, f32[64,256]{1,0:T(8,128)S(1)}, u32[]{:S(2)}, u32[]{:S(2)}) collective-permute-start(f32[64,256]{1,0:T(8,128)S(1)} %add.123), channel_id=1, source_target_pairs={{0,192},{6,198},{12,204},{18,210},{24,216},{30,222},{36,228},{42,2... | collective-permute-start | bytes 196616 | tf_op jit(solution)/shard_map/ppermute | solution.py:78
  144.2 4.0 %collective-permute-done.15 = f32[64,256]{1,0:T(8,128)S(1)} collective-permute-done((f32[64,256]{1,0:T(8,128)S(1)}, f32[64,256]{1,0:T(8,128)S(1)}, u32[]{:S(2)}, u32[]{:S(2)}) %collective-permute-start.15) | collective-permute-done | bytes 65568 | tf_op jit(solution)/shard_map/ppermute | solution.py:78
  148.2 1.9 %collective-permute-start.16 = (f32[64,256]{1,0:T(8,128)S(1)}, f32[64,256]{1,0:T(8,128)S(1)}, u32[]{:S(2)}, u32[]{:S(2)}) collective-permute-start(f32[64,256]{1,0:T(8,128)S(1)} %add.124), channel_id=1, source_target_pairs={{0,384},{6,390},{12,396},{18,402},{24,408},{30,414},{36,420},{42,4... | collective-permute-start | bytes 196616 | tf_op jit(solution)/shard_map/ppermute | solution.py:78
  150.2 1.7 %fusion.23 = bf16[192,256]{1,0:T(8,128)(2,1)} fusion(f32[1152,256]{1,0:T(8,128)} %get-tuple-element.24, s32[]{:T(128)S(6)} %select_n.150, f32[1152,256]{1,0:T(8,128)} %get-tuple-element.34), kind=kLoop, calls=%fused_computation.29 | loop fusion | flops 98304 | bytes 491524 | tf_op jit(solution)/shard_map/convert_element_type | solution.py:68
  151.9 2.9 %collective-permute-done.16 = f32[64,256]{1,0:T(8,128)S(1)} collective-permute-done((f32[64,256]{1,0:T(8,128)S(1)}, f32[64,256]{1,0:T(8,128)S(1)}, u32[]{:S(2)}, u32[]{:S(2)}) %collective-permute-start.16) | collective-permute-done | bytes 65568 | tf_op jit(solution)/shard_map/ppermute | solution.py:78
  154.8 3.5 %collective-permute-start.17 = (f32[64,256]{1,0:T(8,128)S(1)}, f32[64,256]{1,0:T(8,128)S(1)}, u32[]{:S(2)}, u32[]{:S(2)}) collective-permute-start(f32[64,256]{1,0:T(8,128)S(1)} %add_multiply_fusion), channel_id=1, source_target_pairs={{0,1},{1,0},{2,3},{3,2},{4,5},{5,4},{6,7},{7,6},{8,9},{9,8},{10,11... | collective-permute-start | bytes 196616 | tf_op jit(solution)/shard_map/ppermute | solution.py:28
  158.2 0.7 multiply_convert_fusion.3
  159.0 0.2 collective-permute-done.17
  159.1 0.7 pad_maximum_fusion.1
  (34 shorter events, 1.0 us)
Async XLA Ops:
  0.6 30.6 %copy-start = (bf16[1,1152,1152]{2,1,0:T(8,128)(2,1)S(1)}, bf16[1,1152,1152]{2,1,0:T(8,128)(2,1)}, u32[]{:S(2)}) copy-start(bf16[1,1152,1152]{2,1,0:T(8,128)(2,1)} %param.8) | copy-start | bytes 7962628
  2.7 16.1 %collective-permute-start = (bf16[576,128]{1,0:T(8,128)(2,1)S(1)}, bf16[576,128]{1,0:T(8,128)(2,1)S(1)}, u32[]{:S(2)}, u32[]{:S(2)}) collective-permute-start(bf16[576,128]{1,0:T(8,128)(2,1)S(1)} %multiply_convert_fusion.2), channel_id=1, source_target_pairs={{0,0},{1,7},{2,14},{3,21},{4,28},{5,35},{6,6},{7,13},{8,20},{9,27}... | collective-permute-start | bytes 442376 | tf_op jit(solution)/shard_map/ppermute | solution.py:25
  18.7 12.5 %collective-permute-start.1 = (bf16[576,128]{1,0:T(8,128)(2,1)S(1)}, bf16[576,128]{1,0:T(8,128)(2,1)S(1)}, u32[]{:S(2)}, u32[]{:S(2)}) collective-permute-start(bf16[576,128]{1,0:T(8,128)(2,1)S(1)} %collective-permute-done), channel_id=1, source_target_pairs={{0,7},{1,762},{2,9},{3,764},{4,11},{5,766},{6,13},{7,0},{8,15},{9,... | collective-permute-start | bytes 442376 | tf_op jit(solution)/shard_map/ppermute | solution.py:25
  34.3 3.3 %collective-permute-start.2 = (bf16[3,192,128]{2,1,0:T(8,128)(2,1)S(1)}, bf16[3,192,128]{2,1,0:T(8,128)(2,1)S(1)}, u32[]{:S(2)}, u32[]{:S(2)}) collective-permute-start(bf16[3,192,128]{2,1,0:T(8,128)(2,1)S(1)} %fusion.24), channel_id=1, source_target_pairs={{0,1},{1,0},{2,3},{3,2},{4,5},{5,4},{6,7},{7,6},{8,9},{9,8},{10,11... | collective-permute-start | bytes 442376 | tf_op jit(solution)/shard_map/ppermute | solution.py:28
  38.5 27.3 %collective-permute-start.3 = (bf16[3,192,128]{2,1,0:T(8,128)(2,1)S(1)}, bf16[3,192,128]{2,1,0:T(8,128)(2,1)S(1)}, u32[]{:S(2)}, u32[]{:S(2)}) collective-permute-start(bf16[3,192,128]{2,1,0:T(8,128)(2,1)S(1)} %fusion.21), channel_id=1, source_target_pairs={{0,2},{1,3},{2,4},{3,5},{4,0},{5,1},{6,8},{7,9},{8,10},{9,11},{10,... | collective-permute-start | bytes 442376 | tf_op jit(solution)/shard_map/ppermute | solution.py:53
  54.4 14.6 %collective-permute-start.4 = (bf16[3,192,128]{2,1,0:T(8,128)(2,1)S(1)}, bf16[3,192,128]{2,1,0:T(8,128)(2,1)S(1)}, u32[]{:S(2)}, u32[]{:S(2)}) collective-permute-start(bf16[3,192,128]{2,1,0:T(8,128)(2,1)S(1)} %fusion.21), channel_id=1, source_target_pairs={{0,4},{1,5},{2,0},{3,1},{4,2},{5,3},{6,10},{7,11},{8,6},{9,7},{10,... | collective-permute-start | bytes 442376 | tf_op jit(solution)/shard_map/ppermute | solution.py:54
  69.1 3.8 %copy-start.2 = (bf16[128,256]{1,0:T(8,128)(2,1)S(1)}, bf16[128,256]{1,0:T(8,128)(2,1)}, u32[]{:S(2)}) copy-start(bf16[128,256]{1,0:T(8,128)(2,1)} %param.10) | copy-start | bytes 196612
  69.3 3.4 %collective-permute-start.5 = (bf16[576,128]{1,0:T(8,128)(2,1)S(1)}, bf16[576,128]{1,0:T(8,128)(2,1)S(1)}, u32[]{:S(2)}, u32[]{:S(2)}) collective-permute-start(bf16[576,128]{1,0:T(8,128)(2,1)S(1)} %fusion.20), channel_id=1, source_target_pairs={{0,1},{1,0},{2,3},{3,2},{4,5},{5,4},{6,7},{7,6},{8,9},{9,8},{10,11... | collective-permute-start | bytes 442376 | tf_op jit(solution)/shard_map/ppermute | solution.py:28
  71.7 1.2 copy-start.3
  74.8 0.8 copy-start.1
  78.0 5.0 %collective-permute-start.6 = (f32[64,256]{1,0:T(8,128)S(1)}, f32[64,256]{1,0:T(8,128)S(1)}, u32[]{:S(2)}, u32[]{:S(2)}) collective-permute-start(f32[64,256]{1,0:T(8,128)S(1)} %constant_dynamic-slice_fusion), channel_id=1, source_target_pairs={{0,6},{6,0},{12,18},{18,12},{24,30},{30,24},{36,42},{42,36},{48,54... | collective-permute-start | bytes 196616 | tf_op jit(solution)/shard_map/ppermute | solution.py:78
  83.1 20.1 %collective-permute-start.8 = (bf16[3,192,128]{2,1,0:T(8,128)(2,1)S(1)}, bf16[3,192,128]{2,1,0:T(8,128)(2,1)S(1)}, u32[]{:S(2)}, u32[]{:S(2)}) collective-permute-start(bf16[3,192,128]{2,1,0:T(8,128)(2,1)S(1)} %fusion.25), channel_id=1, source_target_pairs={{0,7},{1,762},{2,9},{3,764},{4,11},{5,766},{6,13},{7,0},{8,15},{9,... | collective-permute-start | bytes 442376 | tf_op jit(solution)/shard_map/ppermute | solution.py:25
  95.4 7.7 %collective-permute-start.7 = (f32[64,256]{1,0:T(8,128)S(1)}, f32[64,256]{1,0:T(8,128)S(1)}, u32[]{:S(2)}, u32[]{:S(2)}) collective-permute-start(f32[64,256]{1,0:T(8,128)S(1)} %fusion.35), channel_id=1, source_target_pairs={{0,12},{6,18},{12,0},{18,6},{24,36},{30,42},{36,24},{42,30},{48,60... | collective-permute-start | bytes 196616 | tf_op jit(solution)/shard_map/ppermute | solution.py:78
  103.2 8.9 %collective-permute-start.9 = (f32[64,256]{1,0:T(8,128)S(1)}, f32[64,256]{1,0:T(8,128)S(1)}, u32[]{:S(2)}, u32[]{:S(2)}) collective-permute-start(f32[64,256]{1,0:T(8,128)S(1)} %add.109), channel_id=1, source_target_pairs={{0,24},{6,30},{12,36},{18,42},{24,0},{30,6},{36,12},{42,18},{48,72... | collective-permute-start | bytes 196616 | tf_op jit(solution)/shard_map/ppermute | solution.py:78
  112.1 13.6 %collective-permute-start.10 = (f32[64,256]{1,0:T(8,128)S(1)}, f32[64,256]{1,0:T(8,128)S(1)}, u32[]{:S(2)}, u32[]{:S(2)}) collective-permute-start(f32[64,256]{1,0:T(8,128)S(1)} %add.111), channel_id=1, source_target_pairs={{0,48},{6,54},{12,60},{18,66},{24,72},{30,78},{36,84},{42,90},{48,... | collective-permute-start | bytes 196616 | tf_op jit(solution)/shard_map/ppermute | solution.py:78
  114.0 11.6 %collective-permute-start.11 = (bf16[192,128]{1,0:T(8,128)(2,1)S(1)}, bf16[192,128]{1,0:T(8,128)(2,1)S(1)}, u32[]{:S(2)}, u32[]{:S(2)}) collective-permute-start(bf16[192,128]{1,0:T(8,128)(2,1)S(1)} %get-tuple-element.31), channel_id=1, source_target_pairs={{0,0},{1,763},{2,758},{3,753},{4,748},{5,743},{6,6},{7,1},{8,764},... | collective-permute-start | bytes 147464 | tf_op jit(solution)/shard_map/ppermute | solution.py:25
  116.5 13.5 %collective-permute-start.12 = (bf16[192,128]{1,0:T(8,128)(2,1)S(1)}, bf16[192,128]{1,0:T(8,128)(2,1)S(1)}, u32[]{:S(2)}, u32[]{:S(2)}) collective-permute-start(bf16[192,128]{1,0:T(8,128)(2,1)S(1)} %get-tuple-element.30), channel_id=1, source_target_pairs={{0,2},{1,765},{2,760},{3,755},{4,744},{5,739},{6,8},{7,3},{8,766},... | collective-permute-start | bytes 147464 | tf_op jit(solution)/shard_map/ppermute | solution.py:25
  123.7 12.6 %collective-permute-start.13 = (bf16[192,128]{1,0:T(8,128)(2,1)S(1)}, bf16[192,128]{1,0:T(8,128)(2,1)S(1)}, u32[]{:S(2)}, u32[]{:S(2)}) collective-permute-start(bf16[192,128]{1,0:T(8,128)(2,1)S(1)} %get-tuple-element.29), channel_id=1, source_target_pairs={{0,4},{1,767},{2,756},{3,751},{4,746},{5,741},{6,10},{7,5},{8,762}... | collective-permute-start | bytes 147464 | tf_op jit(solution)/shard_map/ppermute | solution.py:25
  136.3 5.9 %collective-permute-start.14 = (f32[64,256]{1,0:T(8,128)S(1)}, f32[64,256]{1,0:T(8,128)S(1)}, u32[]{:S(2)}, u32[]{:S(2)}) collective-permute-start(f32[64,256]{1,0:T(8,128)S(1)} %add.112), channel_id=1, source_target_pairs={{0,96},{6,102},{12,108},{18,114},{24,120},{30,126},{36,132},{42,13... | collective-permute-start | bytes 196616 | tf_op jit(solution)/shard_map/ppermute | solution.py:78
  142.2 6.0 %collective-permute-start.15 = (f32[64,256]{1,0:T(8,128)S(1)}, f32[64,256]{1,0:T(8,128)S(1)}, u32[]{:S(2)}, u32[]{:S(2)}) collective-permute-start(f32[64,256]{1,0:T(8,128)S(1)} %add.123), channel_id=1, source_target_pairs={{0,192},{6,198},{12,204},{18,210},{24,216},{30,222},{36,228},{42,2... | collective-permute-start | bytes 196616 | tf_op jit(solution)/shard_map/ppermute | solution.py:78
  148.2 6.5 %collective-permute-start.16 = (f32[64,256]{1,0:T(8,128)S(1)}, f32[64,256]{1,0:T(8,128)S(1)}, u32[]{:S(2)}, u32[]{:S(2)}) collective-permute-start(f32[64,256]{1,0:T(8,128)S(1)} %add.124), channel_id=1, source_target_pairs={{0,384},{6,390},{12,396},{18,402},{24,408},{30,414},{36,420},{42,4... | collective-permute-start | bytes 196616 | tf_op jit(solution)/shard_map/ppermute | solution.py:78
  154.8 4.3 %collective-permute-start.17 = (f32[64,256]{1,0:T(8,128)S(1)}, f32[64,256]{1,0:T(8,128)S(1)}, u32[]{:S(2)}, u32[]{:S(2)}) collective-permute-start(f32[64,256]{1,0:T(8,128)S(1)} %add_multiply_fusion), channel_id=1, source_target_pairs={{0,1},{1,0},{2,3},{3,2},{4,5},{5,4},{6,7},{7,6},{8,9},{9,8},{10,11... | collective-permute-start | bytes 196616 | tf_op jit(solution)/shard_map/ppermute | solution.py:28

commit v3 on v2

--- a/solution.py
+++ b/solution.py
@@ -27,9 +27,6 @@
     def swap_core(value):
         return lax.ppermute(value, "rep", [(s, s ^ 1) for s in range(reps)])
 
-    def pair_move(i, s):
-        return (i + 1 if s % 2 == 0 else i - 1, s ^ 1)
-
     def pick(array, which):
         return lax.dynamic_index_in_dim(array, which, 1, keepdims=False)
 
@@ -40,11 +37,7 @@
     tile_on = pattern[0, 0].astype(F32)
     tile = tiles[0]
 
-    mid = rows // 2
-    sent = lax.dynamic_slice_in_dim(source, core * mid, mid, 0)
-    held = across(sent, lambda i, s: (i + s, s))
-    other = across(held, pair_move)
-    block = jnp.concatenate([jnp.where(core == 0, held, other), jnp.where(core == 0, other, held)], axis=0)
+    block = across(source, lambda i, s: (i + s, s))
     partial = jnp.dot(tile, block, preferred_element_type=F32) * tile_on
     parts = partial.reshape(zs, 2, own, feat)
 
@@ -72,37 +65,38 @@
     ).astype(BF)
     grad_part = lax.dot_general(aggregated, slope, (((0,), (0,)), ((), ())), preferred_element_type=F32)
 
-    grad = lax.dynamic_slice_in_dim(grad_part, core * (feat // 2), feat // 2, 0)
+    back = lax.dot_general(tile, message, (((0,), (0,)), ((), ())), preferred_element_type=F32) * tile_on
+    back = back.astype(BF)
 
-    def pair_sum(value, bit):
-        return value + lax.ppermute(value, "team", [(i, i ^ bit) for i in range(teams)])
+    lanes = hid // 2
+    size = -(-2 * feat // (16 * reps)) * 16
+    tall = jnp.concatenate(
+        [grad_part[:, :lanes], grad_part[:, lanes:], jnp.zeros((reps * size - 2 * feat, lanes), F32)], axis=0
+    )
+    piece = lax.dynamic_slice_in_dim(tall, rep * size, size, 0)
+    piece, back = lax.optimization_barrier((piece, back))
+    returned = across(back, lambda i, s: (i - s, s))
+    inner = math.gcd(teams, 8)
+    bit = 1
+    while bit < inner:
+        piece = piece + lax.ppermute(piece, "team", [(i, i ^ bit) for i in range(teams)])
+        bit *= 2
+    piece, returned = lax.optimization_barrier((piece, returned))
+    groups = [[b * inner + y for b in range(teams // inner)] for y in range(inner)]
+    spread = jnp.broadcast_to(piece[None], (len(groups[0]), size, lanes))
+    piece = lax.all_to_all(spread, "team", 0, 0, axis_index_groups=groups).sum(axis=0)
+    piece = piece * (1.0 / math.sqrt(rows * teams))
 
-    bits = [1 << b for b in range((teams - 1).bit_length())]
-    grad = pair_sum(grad, bits[0])
-    back = lax.dot_general(tile, message, (((0,), (0,)), ((), ())), preferred_element_type=F32) * tile_on
-    backs = back.reshape(zs, 2, own, feat)
-    keep, give = pick(backs, core), pick(backs, 1 - core).astype(BF)
-    grad, keep, give = lax.optimization_barrier((grad, keep, give))
-    taken = across(give, pair_move)
-    grad = pair_sum(grad, bits[1])
-    sent = (keep + taken.astype(F32)).astype(BF)
-    grad, sent = lax.optimization_barrier((grad, sent))
-    got = []
-    for k in range(zs):
-        chunk = lax.dynamic_index_in_dim(sent, (z + k) % zs, 0, keepdims=False)
-        got.append(across(chunk, lambda i, s: (i - s, 2 * ((s // 2 + k) % zs) + s % 2)))
-    for bit in bits[2:4]:
-        grad = pair_sum(grad, bit)
-    grad, got = lax.optimization_barrier((grad, got))
-    summed = sum(g.astype(F32) for g in got)
+    high = lax.reduce_precision(piece, 8, 7)
+    packed = jnp.concatenate([high.astype(BF), (piece - high).astype(BF)], axis=0)
+    payload = jnp.concatenate(
+        [returned.reshape(reps, own, feat), jnp.broadcast_to(packed[None], (reps, 2 * size, lanes))], axis=1
+    )
+    got = lax.all_to_all(payload, "rep", 0, 0)
+    summed = got[:, :own].astype(F32).sum(axis=0)
     grad_features = (summed * inv_own[:, None]).astype(BF)
-    for bit in bits[4:]:
-        grad = pair_sum(grad, bit)
-    grad = grad * (1.0 / math.sqrt(rows * teams))
-    grad_other = swap_core(grad)
-    grad_weight = jnp.concatenate(
-        [jnp.where(core == 0, grad, grad_other), jnp.where(core == 0, grad_other, grad)], axis=0
-    )
+    tall = (got[:, own : own + size].astype(F32) + got[:, own + size :].astype(F32)).reshape(reps * size, lanes)
+    grad_weight = jnp.concatenate([tall[:feat], tall[feat : 2 * feat]], axis=1)
     return (hidden, grad_features, grad_weight)
 
 

time: 161 us -> 162 us (level)
  starting transfers between devices: 68.9 us -> 72.3 us
  local copies, waits for them, and re-layouts: 6.34 us -> 4.41 us
    all_to_all x0 -> x2, waiting for transfers between devices: none -> 27.8 us  [the longest x1 16.1 us: local(): got = lax.all_to_all(payload, 'rep', 0, 0)]
    all_to_all x0 -> x2, starting transfers between devices: none -> 23.4 us  [the longest x1 19.9 us: local(): got = lax.all_to_all(payload, 'rep', 0, 0)]
    ppermute x6 -> x2, waiting for transfers between devices: 32.6 us -> 12.9 us  [across(): return lax.ppermute(value, ('team', 'rep'), route)]
    ppermute x6 -> x2, starting transfers between devices: 29.9 us -> 11.5 us  [across(): return lax.ppermute(value, ('team', 'rep'), route)]
    ppermute x7 -> x3, waiting for transfers between devices: 23.6 us -> 12.3 us  [local(): lax.ppermute(piece, 'team', [(i, i ^ bit) for i in range(teams)])]
    ppermute x1, starting transfers between devices: 15.9 us -> 23.3 us  [local(): lax.ppermute(sent, 'rep', [(s, (s + 2) % reps) for s in range(reps)])]
    ppermute x7 -> x3, starting transfers between devices: 13.4 us -> 6.2 us  [local(): lax.ppermute(piece, 'team', [(i, i ^ bit) for i in range(teams)])]
    ppermute x1, waiting for transfers between devices: 3.21 us -> 7.73 us  [local(): lax.ppermute(sent, 'rep', [(s, (s + 4) % reps) for s in range(reps)])]
  transfers between devices with their start and end apart: 18 -> 11, of which waited for: 14 -> 10; matrix products, arithmetic and copies ran while one was open for 4% -> 2% of each run, Pallas kernels for 0% -> 0%
where the time goes in v3:
time: 162 us; the launch traced here: 161 us
  starting transfers between devices  72.3 us (45%)
  waiting for transfers between devices  70 us (43%)
  other arithmetic  7.49 us (5%)
  matrix products  4.87 us (3%)
  local copies, waits for them, and re-layouts  4.41 us (3%)
  between operations  1.62 us (1%)
    ppermute x1, starting transfers between devices, local(): lax.ppermute(sent, 'rep', [(s, (s + 2) % reps) for s in range(reps)])  23.3 us
    all_to_all x1, starting transfers between devices, local(): got = lax.all_to_all(payload, 'rep', 0, 0)  19.9 us
    all_to_all x1, waiting for transfers between devices, local(): got = lax.all_to_all(payload, 'rep', 0, 0)  16.1 us
    ppermute x2, waiting for transfers between devices, across(): return lax.ppermute(value, ('team', 'rep'), route)  12.9 us
    ppermute x3, waiting for transfers between devices, local(): lax.ppermute(piece, 'team', [(i, i ^ bit) for i in range(teams)])  12.3 us
    all_to_all x1, waiting for transfers between devices, local(): lax.all_to_all(spread, 'team', 0, 0, axis_index_groups=groups).sum(axis=0)  11.7 us
    ppermute x2, starting transfers between devices, across(): return lax.ppermute(value, ('team', 'rep'), route)  11.5 us
    ppermute x1, waiting for transfers between devices, local(): lax.ppermute(sent, 'rep', [(s, (s + 4) % reps) for s in range(reps)])  7.73 us
  transfers between devices with their start and end apart: 11, of which 10 were waited for; matrix products, arithmetic and copies ran while one was open for 2% of the time, Pallas kernels for 0%

profile of v3, /device:TPU:1, one launch (start us, length us, event | category | flops | bytes accessed | tf_op | source)
XLA Modules:
  0.0 160.7 jit_solution(5848969185560568529)
XLA Ops:
  0.6 0.0 copy-start
  0.6 0.9 convert_rsqrt_fusion
  1.5 1.2 multiply_convert_fusion.1
  2.7 4.0 %collective-permute-start = (bf16[1152,128]{1,0:T(8,128)(2,1)S(1)}, bf16[1152,128]{1,0:T(8,128)(2,1)S(1)}, u32[]{:S(2)}, u32[]{:S(2)}) collective-permute-start(bf16[1152,128]{1,0:T(8,128)(2,1)S(1)} %multiply_convert_fusion.1), channel_id=1, source_target_pairs={{0,0},{1,7},{2,14},{3,21},{4,28},{5,35},{6,6},{7,13},{8,20},{9,27}... | collective-permute-start | bytes 884744 | tf_op jit(solution)/shard_map/ppermute | solution.py:25
  7.4 12.9 %collective-permute-done = bf16[1152,128]{1,0:T(8,128)(2,1)S(1)} collective-permute-done((bf16[1152,128]{1,0:T(8,128)(2,1)S(1)}, bf16[1152,128]{1,0:T(8,128)(2,1)S(1)}, u32[]{:S(2)}, u32[]{:S(2)}) %collective-permute-start) | collective-permute-done | bytes 294944 | tf_op jit(solution)/shard_map/ppermute | solution.py:25
  20.3 1.0 fusion.10
  21.3 1.1 copy.13
  22.4 1.0 fusion.24
  23.3 1.9 %collective-permute-start.1 = (bf16[3,192,128]{2,1,0:T(8,128)(2,1)S(1)}, bf16[3,192,128]{2,1,0:T(8,128)(2,1)S(1)}, u32[]{:S(2)}, u32[]{:S(2)}) collective-permute-start(bf16[3,192,128]{2,1,0:T(8,128)(2,1)S(1)} %fusion.24), channel_id=1, source_target_pairs={{0,1},{1,0},{2,3},{3,2},{4,5},{5,4},{6,7},{7,6},{8,9},{9,8},{10,11... | collective-permute-start | bytes 442376 | tf_op jit(solution)/shard_map/ppermute | solution.py:28
  25.3 1.3 collective-permute-done.1
  26.6 1.0 fusion.21
  27.6 23.3 %collective-permute-start.2 = (bf16[3,192,128]{2,1,0:T(8,128)(2,1)S(1)}, bf16[3,192,128]{2,1,0:T(8,128)(2,1)S(1)}, u32[]{:S(2)}, u32[]{:S(2)}) collective-permute-start(bf16[3,192,128]{2,1,0:T(8,128)(2,1)S(1)} %fusion.21), channel_id=1, source_target_pairs={{0,2},{1,3},{2,4},{3,5},{4,0},{5,1},{6,8},{7,9},{8,10},{9,11},{10,... | collective-permute-start | bytes 442376 | tf_op jit(solution)/shard_map/ppermute | solution.py:46
  51.0 3.5 %collective-permute-start.3 = (bf16[3,192,128]{2,1,0:T(8,128)(2,1)S(1)}, bf16[3,192,128]{2,1,0:T(8,128)(2,1)S(1)}, u32[]{:S(2)}, u32[]{:S(2)}) collective-permute-start(bf16[3,192,128]{2,1,0:T(8,128)(2,1)S(1)} %fusion.21), channel_id=1, source_target_pairs={{0,4},{1,5},{2,0},{3,1},{4,2},{5,3},{6,10},{7,11},{8,6},{9,7},{10,... | collective-permute-start | bytes 442376 | tf_op jit(solution)/shard_map/ppermute | solution.py:47
  54.5 0.1 reshape.53
  54.6 0.1 mul.87
  54.7 7.1 %collective-permute-done.2 = bf16[3,192,128]{2,1,0:T(8,128)(2,1)S(1)} collective-permute-done((bf16[3,192,128]{2,1,0:T(8,128)(2,1)S(1)}, bf16[3,192,128]{2,1,0:T(8,128)(2,1)S(1)}, u32[]{:S(2)}, u32[]{:S(2)}) %collective-permute-start.2) | collective-permute-done | bytes 147488 | tf_op jit(solution)/shard_map/ppermute | solution.py:46
  61.8 7.7 %collective-permute-done.3 = bf16[3,192,128]{2,1,0:T(8,128)(2,1)S(1)} collective-permute-done((bf16[3,192,128]{2,1,0:T(8,128)(2,1)S(1)}, bf16[3,192,128]{2,1,0:T(8,128)(2,1)S(1)}, u32[]{:S(2)}, u32[]{:S(2)}) %collective-permute-start.3) | collective-permute-done | bytes 147488 | tf_op jit(solution)/shard_map/ppermute | solution.py:47
  69.5 0.1 convert_add_fusion
  69.6 0.0 copy-start.1
  69.6 0.1 fusion.20
  69.8 2.4 %collective-permute-start.4 = (bf16[576,128]{1,0:T(8,128)(2,1)S(1)}, bf16[576,128]{1,0:T(8,128)(2,1)S(1)}, u32[]{:S(2)}, u32[]{:S(2)}) collective-permute-start(bf16[576,128]{1,0:T(8,128)(2,1)S(1)} %fusion.20), channel_id=1, source_target_pairs={{0,1},{1,0},{2,3},{3,2},{4,5},{5,4},{6,7},{7,6},{8,9},{9,8},{10,11... | collective-permute-start | bytes 442376 | tf_op jit(solution)/shard_map/ppermute | solution.py:28
  72.2 0.0 copy-start.2
  72.2 0.1 pad_dynamic-slice_fusion.2
  72.3 0.9 collective-permute-done.4
  73.2 0.1 select_bitcast_fusion.1
  73.4 1.9 %multiply_convert_fusion = (bf16[1152,256]{1,0:T(8,128)(2,1)S(1)}, f32[1152,256]{1,0:T(8,128)}, f32[1152,256]{1,0:T(8,128)}) fusion(bf16[1152,256]{1,0:T(8,128)(2,1)S(1)} %copy-done.2, bf16[1152,128]{1,0:T(8,128)(2,1)S(1)} %bitcast.52, bf16[128,256]{1,0:T(8,128)(2,1)S(1)} %copy-done.1), kind=kOutput, calls=%fused_computation.11 | convolution fusion | flops 78446592 | bytes 3899392 | tf_op jit(solution)/shard_map/dot_general | solution.py:59
  75.3 0.3 fusion.31
  75.6 1.7 %fusion.17 = bf16[1152,128]{0,1:T(8,128)(2,1)} fusion(bf16[1,1152,1152]{2,1,0:T(8,128)(2,1)S(1)} %copy-done, bf16[1152,256]{1,0:T(8,128)(2,1)S(1)} %get-tuple-element.13, bf16[128,256]{1,0:T(8,128)(2,1)S(1)} %copy-done.1, f32[]{:T(128)} %bitcast.1, f32[1152]{0:T(1024)S(1)} %convert_rsqrt_fusion), kind=kOutput, calls=%fused_computation.10 | convolution fusion | flops 415825920 | bytes 3609092 | tf_op jit(solution)/shard_map/dot_general | solution.py:68
  77.3 0.1 fusion.27
  77.4 7.5 %collective-permute-start.8 = (bf16[1152,128]{0,1:T(8,128)(2,1)}, bf16[1152,128]{0,1:T(8,128)(2,1)}, u32[]{:S(2)}, u32[]{:S(2)}) collective-permute-start(bf16[1152,128]{0,1:T(8,128)(2,1)} %fusion.17), channel_id=1, source_target_pairs={{0,0},{1,763},{2,758},{3,753},{4,748},{5,743},{6,6},{7,1},{8,764},... | collective-permute-start | bytes 884744 | tf_op jit(solution)/shard_map/ppermute | solution.py:25
  84.9 1.9 %collective-permute-start.5 = (f32[48,128]{1,0:T(8,128)S(1)}, f32[48,128]{1,0:T(8,128)S(1)}, u32[]{:S(2)}, u32[]{:S(2)}) collective-permute-start(f32[48,128]{1,0:T(8,128)S(1)} %fusion.27), channel_id=1, source_target_pairs={{0,6},{6,0},{12,18},{18,12},{24,30},{30,24},{36,42},{42,36},{48,54... | collective-permute-start | bytes 73736 | tf_op jit(solution)/shard_map/ppermute | solution.py:82
  86.8 2.6 %collective-permute-done.5 = f32[48,128]{1,0:T(8,128)S(1)} collective-permute-done((f32[48,128]{1,0:T(8,128)S(1)}, f32[48,128]{1,0:T(8,128)S(1)}, u32[]{:S(2)}, u32[]{:S(2)}) %collective-permute-start.5) | collective-permute-done | bytes 24608 | tf_op jit(solution)/shard_map/ppermute | solution.py:82
  89.5 1.9 %collective-permute-start.6 = (f32[48,128]{1,0:T(8,128)S(1)}, f32[48,128]{1,0:T(8,128)S(1)}, u32[]{:S(2)}, u32[]{:S(2)}) collective-permute-start(f32[48,128]{1,0:T(8,128)S(1)} %add.59), channel_id=1, source_target_pairs={{0,12},{6,18},{12,0},{18,6},{24,36},{30,42},{36,24},{42,30},{48,60... | collective-permute-start | bytes 73736 | tf_op jit(solution)/shard_map/ppermute | solution.py:82
  91.4 3.5 %collective-permute-done.6 = f32[48,128]{1,0:T(8,128)S(1)} collective-permute-done((f32[48,128]{1,0:T(8,128)S(1)}, f32[48,128]{1,0:T(8,128)S(1)}, u32[]{:S(2)}, u32[]{:S(2)}) %collective-permute-start.6) | collective-permute-done | bytes 24608 | tf_op jit(solution)/shard_map/ppermute | solution.py:82
  94.9 2.4 %collective-permute-start.7 = (f32[48,128]{1,0:T(8,128)S(1)}, f32[48,128]{1,0:T(8,128)S(1)}, u32[]{:S(2)}, u32[]{:S(2)}) collective-permute-start(f32[48,128]{1,0:T(8,128)S(1)} %add.60), channel_id=1, source_target_pairs={{0,24},{6,30},{12,36},{18,42},{24,0},{30,6},{36,12},{42,18},{48,72... | collective-permute-start | bytes 73736 | tf_op jit(solution)/shard_map/ppermute | solution.py:82
  97.3 6.1 %collective-permute-done.7 = f32[48,128]{1,0:T(8,128)S(1)} collective-permute-done((f32[48,128]{1,0:T(8,128)S(1)}, f32[48,128]{1,0:T(8,128)S(1)}, u32[]{:S(2)}, u32[]{:S(2)}) %collective-permute-start.7) | collective-permute-done | bytes 24608 | tf_op jit(solution)/shard_map/ppermute | solution.py:82
  103.4 0.0 collective-permute-done.8
  103.4 0.8 broadcast_in_dim.7
  104.2 3.6 %all-to-all-start = ((f32[16,48,128]{2,1,0:T(8,128)}), f32[16,48,128]{2,1,0:T(8,128)S(1)}, u32[]{:S(2)}, u32[]{:S(2)}) async-start(f32[16,48,128]{2,1,0:T(8,128)} %broadcast_in_dim.7), calls=%async_computation | async-start | bytes 786432 | tf_op jit(solution)/shard_map/all_to_all | solution.py:87
  107.7 1.2 copy.15
  108.9 11.7 %all-to-all-done = f32[16,48,128]{2,1,0:T(8,128)S(1)} async-done(((f32[16,48,128]{2,1,0:T(8,128)}), f32[16,48,128]{2,1,0:T(8,128)S(1)}, u32[]{:S(2)}, u32[]{:S(2)}) %all-to-all-start) | async-done | bytes 393248 | tf_op jit(solution)/shard_map/all_to_all | solution.py:87
  120.7 0.8 pad_maximum_fusion
  121.5 19.9 %all-to-all-start.1 = ((bf16[6,288,128]{2,1,0:T(8,128)(2,1)}), bf16[6,288,128]{2,1,0:T(8,128)(2,1)S(1)}, u32[]{:S(2)}, u32[]{:S(2)}) async-start(bf16[6,288,128]{2,1,0:T(8,128)(2,1)} %pad_maximum_fusion), calls=%async_computation.1 | async-start | bytes 884736 | tf_op jit(solution)/shard_map/all_to_all | solution.py:95
  141.3 0.1 dynamic_slice.25
  141.4 1.7 %fusion.23 = bf16[192,256]{1,0:T(8,128)(2,1)} fusion(f32[1152,256]{1,0:T(8,128)} %get-tuple-element.14, s32[]{:T(128)S(6)} %select_n.95, f32[1152,256]{1,0:T(8,128)} %get-tuple-element.23), kind=kLoop, calls=%fused_computation.26 | loop fusion | flops 98304 | bytes 491524 | tf_op jit(solution)/shard_map/convert_element_type | solution.py:61
  143.1 16.1 %all-to-all-done.1 = bf16[6,288,128]{2,1,0:T(8,128)(2,1)S(1)} async-done(((bf16[6,288,128]{2,1,0:T(8,128)(2,1)}), bf16[6,288,128]{2,1,0:T(8,128)(2,1)S(1)}, u32[]{:S(2)}, u32[]{:S(2)}) %all-to-all-start.1) | async-done | bytes 442400 | tf_op jit(solution)/shard_map/all_to_all | solution.py:95
  159.3 0.7 multiply_convert_fusion.3
  160.0 0.7 pad_maximum_fusion.2
  (19 shorter events, 0.2 us)
Async XLA Ops:
  0.6 19.7 %copy-start = (bf16[1,1152,1152]{2,1,0:T(8,128)(2,1)S(1)}, bf16[1,1152,1152]{2,1,0:T(8,128)(2,1)}, u32[]{:S(2)}) copy-start(bf16[1,1152,1152]{2,1,0:T(8,128)(2,1)} %param.8) | copy-start | bytes 7962628
  2.7 17.7 %collective-permute-start = (bf16[1152,128]{1,0:T(8,128)(2,1)S(1)}, bf16[1152,128]{1,0:T(8,128)(2,1)S(1)}, u32[]{:S(2)}, u32[]{:S(2)}) collective-permute-start(bf16[1152,128]{1,0:T(8,128)(2,1)S(1)} %multiply_convert_fusion.1), channel_id=1, source_target_pairs={{0,0},{1,7},{2,14},{3,21},{4,28},{5,35},{6,6},{7,13},{8,20},{9,27}... | collective-permute-start | bytes 884744 | tf_op jit(solution)/shard_map/ppermute | solution.py:25
  23.3 3.3 %collective-permute-start.1 = (bf16[3,192,128]{2,1,0:T(8,128)(2,1)S(1)}, bf16[3,192,128]{2,1,0:T(8,128)(2,1)S(1)}, u32[]{:S(2)}, u32[]{:S(2)}) collective-permute-start(bf16[3,192,128]{2,1,0:T(8,128)(2,1)S(1)} %fusion.24), channel_id=1, source_target_pairs={{0,1},{1,0},{2,3},{3,2},{4,5},{5,4},{6,7},{7,6},{8,9},{9,8},{10,11... | collective-permute-start | bytes 442376 | tf_op jit(solution)/shard_map/ppermute | solution.py:28
  27.6 34.2 %collective-permute-start.2 = (bf16[3,192,128]{2,1,0:T(8,128)(2,1)S(1)}, bf16[3,192,128]{2,1,0:T(8,128)(2,1)S(1)}, u32[]{:S(2)}, u32[]{:S(2)}) collective-permute-start(bf16[3,192,128]{2,1,0:T(8,128)(2,1)S(1)} %fusion.21), channel_id=1, source_target_pairs={{0,2},{1,3},{2,4},{3,5},{4,0},{5,1},{6,8},{7,9},{8,10},{9,11},{10,... | collective-permute-start | bytes 442376 | tf_op jit(solution)/shard_map/ppermute | solution.py:46
  51.0 18.5 %collective-permute-start.3 = (bf16[3,192,128]{2,1,0:T(8,128)(2,1)S(1)}, bf16[3,192,128]{2,1,0:T(8,128)(2,1)S(1)}, u32[]{:S(2)}, u32[]{:S(2)}) collective-permute-start(bf16[3,192,128]{2,1,0:T(8,128)(2,1)S(1)} %fusion.21), channel_id=1, source_target_pairs={{0,4},{1,5},{2,0},{3,1},{4,2},{5,3},{6,10},{7,11},{8,6},{9,7},{10,... | collective-permute-start | bytes 442376 | tf_op jit(solution)/shard_map/ppermute | solution.py:47
  69.6 3.8 %copy-start.1 = (bf16[128,256]{1,0:T(8,128)(2,1)S(1)}, bf16[128,256]{1,0:T(8,128)(2,1)}, u32[]{:S(2)}) copy-start(bf16[128,256]{1,0:T(8,128)(2,1)} %param.10) | copy-start | bytes 196612
  69.8 3.4 %collective-permute-start.4 = (bf16[576,128]{1,0:T(8,128)(2,1)S(1)}, bf16[576,128]{1,0:T(8,128)(2,1)S(1)}, u32[]{:S(2)}, u32[]{:S(2)}) collective-permute-start(bf16[576,128]{1,0:T(8,128)(2,1)S(1)} %fusion.20), channel_id=1, source_target_pairs={{0,1},{1,0},{2,3},{3,2},{4,5},{5,4},{6,7},{7,6},{8,9},{9,8},{10,11... | collective-permute-start | bytes 442376 | tf_op jit(solution)/shard_map/ppermute | solution.py:28
  72.2 1.2 copy-start.2
  77.4 26.0 %collective-permute-start.8 = (bf16[1152,128]{0,1:T(8,128)(2,1)}, bf16[1152,128]{0,1:T(8,128)(2,1)}, u32[]{:S(2)}, u32[]{:S(2)}) collective-permute-start(bf16[1152,128]{0,1:T(8,128)(2,1)} %fusion.17), channel_id=1, source_target_pairs={{0,0},{1,763},{2,758},{3,753},{4,748},{5,743},{6,6},{7,1},{8,764},... | collective-permute-start | bytes 884744 | tf_op jit(solution)/shard_map/ppermute | solution.py:25
  84.9 4.6 %collective-permute-start.5 = (f32[48,128]{1,0:T(8,128)S(1)}, f32[48,128]{1,0:T(8,128)S(1)}, u32[]{:S(2)}, u32[]{:S(2)}) collective-permute-start(f32[48,128]{1,0:T(8,128)S(1)} %fusion.27), channel_id=1, source_target_pairs={{0,6},{6,0},{12,18},{18,12},{24,30},{30,24},{36,42},{42,36},{48,54... | collective-permute-start | bytes 73736 | tf_op jit(solution)/shard_map/ppermute | solution.py:82
  89.5 5.5 %collective-permute-start.6 = (f32[48,128]{1,0:T(8,128)S(1)}, f32[48,128]{1,0:T(8,128)S(1)}, u32[]{:S(2)}, u32[]{:S(2)}) collective-permute-start(f32[48,128]{1,0:T(8,128)S(1)} %add.59), channel_id=1, source_target_pairs={{0,12},{6,18},{12,0},{18,6},{24,36},{30,42},{36,24},{42,30},{48,60... | collective-permute-start | bytes 73736 | tf_op jit(solution)/shard_map/ppermute | solution.py:82
  94.9 8.5 %collective-permute-start.7 = (f32[48,128]{1,0:T(8,128)S(1)}, f32[48,128]{1,0:T(8,128)S(1)}, u32[]{:S(2)}, u32[]{:S(2)}) collective-permute-start(f32[48,128]{1,0:T(8,128)S(1)} %add.60), channel_id=1, source_target_pairs={{0,24},{6,30},{12,36},{18,42},{24,0},{30,6},{36,12},{42,18},{48,72... | collective-permute-start | bytes 73736 | tf_op jit(solution)/shard_map/ppermute | solution.py:82
  104.2 16.4 %all-to-all-start = ((f32[16,48,128]{2,1,0:T(8,128)}), f32[16,48,128]{2,1,0:T(8,128)S(1)}, u32[]{:S(2)}, u32[]{:S(2)}) async-start(f32[16,48,128]{2,1,0:T(8,128)} %broadcast_in_dim.7), calls=%async_computation | async-start | bytes 786432 | tf_op jit(solution)/shard_map/all_to_all | solution.py:87
  121.5 37.7 %all-to-all-start.1 = ((bf16[6,288,128]{2,1,0:T(8,128)(2,1)}), bf16[6,288,128]{2,1,0:T(8,128)(2,1)S(1)}, u32[]{:S(2)}, u32[]{:S(2)}) async-start(bf16[6,288,128]{2,1,0:T(8,128)(2,1)} %pad_maximum_fusion), calls=%async_computation.1 | async-start | bytes 884736 | tf_op jit(solution)/shard_map/all_to_all | solution.py:95

commit v4 on v3

v4 whole, which is shorter than its diff:
```python
import functools
import math

import jax
import jax.numpy as jnp
from jax import lax
from jax.experimental import pallas as pl
from jax.experimental.pallas import tpu as pltpu
from jax.sharding import PartitionSpec as P

BF = jnp.bfloat16
F32 = jnp.float32


def forward_kernel(own, here_ref, tile_ref, block_ref, keep_ref, give_ref):
    core, tile_on = here_ref[0], here_ref[2].astype(F32)
    for q in range(keep_ref.shape[0]):
        for out_ref, side in ((keep_ref, core), (give_ref, 1 - core)):
            start = pl.multiple_of((2 * q + side) * own, own)
            term = jnp.dot(tile_ref[pl.ds(start, own), :], block_ref[...], preferred_element_type=F32)
            out_ref[q] = (term * tile_on).astype(out_ref.dtype)


def middle_kernel(
    own, size, here_ref, tile_ref, half_ref, other_ref, cot_ref, weight_ref, inv_ref,
    hidden_ref, keep_ref, give_ref, spread_ref, agg, slope, back, tall,
):
    core, rep, tile_on = here_ref[0], here_ref[1], here_ref[2].astype(F32)
    rows, feat = agg.shape
    lanes = tall.shape[1]
    zs = rows // (2 * own)
    weight = weight_ref[...]
    for q in range(zs):
        for in_ref, side in ((half_ref, core), (other_ref, 1 - core)):
            agg[pl.ds(pl.multiple_of((2 * q + side) * own, own), own), :] = in_ref[q * own : (q + 1) * own, :]
    grad = jnp.zeros((feat, weight.shape[1]), F32)
    for q in range(2 * zs):
        part = agg[q * own : (q + 1) * own, :]
        pre_act = jnp.dot(part, weight, preferred_element_type=F32)
        sig = jax.nn.sigmoid(pre_act)
        cot = cot_ref[q * own : (q + 1) * own, :].astype(F32)
        term = (cot * (sig * (1.0 + pre_act * (1.0 - sig)))).astype(BF)
        slope[q * own : (q + 1) * own, :] = term
        grad = grad + lax.dot_general(part, term, (((0,), (0,)), ((), ())), preferred_element_type=F32)
    message = lax.dot_general(weight, slope[...], (((1,), (1,)), ((), ())), preferred_element_type=F32)
    message = (message * inv_ref[...]).astype(BF)
    back[...] = (jnp.dot(message, tile_ref[...], preferred_element_type=F32) * tile_on).T
    for q in range(zs):
        for out_ref, side in ((keep_ref, core), (give_ref, 1 - core)):
            start = pl.multiple_of((2 * q + side) * own, own)
            out_ref[q] = back[pl.ds(start, own), :].astype(out_ref.dtype)
    tall[:feat, :] = grad[:, :lanes]
    tall[feat : 2 * feat, :] = grad[:, lanes:]
    tall[2 * feat :, :] = jnp.zeros((tall.shape[0] - 2 * feat, lanes), F32)
    piece = tall[pl.ds(pl.multiple_of(rep * size, size), size), :]
    for q in range(spread_ref.shape[0]):
        spread_ref[q] = piece
    pre_act = jnp.dot(agg[pl.ds(pl.multiple_of(rep * own, own), own), :], weight, preferred_element_type=F32)
    hidden_ref[...] = (pre_act * jax.nn.sigmoid(pre_act)).astype(BF)


def in_vmem(body, outs, scratch=()):
    def call(here, *arrays):
        vmem = pl.BlockSpec(memory_space=pltpu.VMEM)
        return pl.pallas_call(
            body,
            out_shape=[jax.ShapeDtypeStruct(shape, dtype) for shape, dtype in outs],
            in_specs=[pl.BlockSpec(memory_space=pltpu.SMEM)] + [vmem] * len(arrays),
            out_specs=[vmem] * len(outs),
            scratch_shapes=[pltpu.VMEM(shape, dtype) for shape, dtype in scratch],
            compiler_params=pltpu.CompilerParams(vmem_limit_bytes=10 * 2**20),
        )(here, *arrays)

    return call


def local(features, degrees, tiles, pattern, weight, cotangent):
    teams = lax.axis_size("team")
    reps = lax.axis_size("rep")
    zs = reps // 2
    rep = lax.axis_index("rep")
    z, core = rep // 2, rep % 2
    rows, feat = features.shape
    hid = weight.shape[1]
    own = rows // reps
    half = zs * own

    def across(value, move):
        route = [(i * reps + s, (move(i, s)[0] % teams) * reps + move(i, s)[1]) for i in range(teams) for s in range(reps)]
        return lax.ppermute(value, ("team", "rep"), route)

    def swap_core(value):
        return lax.ppermute(value, "rep", [(s, s ^ 1) for s in range(reps)])

    def pick(array, which):
        return lax.dynamic_index_in_dim(array, which, 1, keepdims=False)

    inv_root = 1.0 / jnp.sqrt(degrees.astype(F32))
    inv_half = pick(inv_root.reshape(zs, 2, own), core).reshape(half)
    inv_own = lax.dynamic_slice_in_dim(inv_root, rep * own, own, 0)
    source = (features.astype(F32) * inv_root[:, None]).astype(BF)
    tile = tiles[0]

    block = across(source, lambda i, s: (i + s, s))
    here = jnp.stack([core, rep, pattern[0, 0]]).astype(jnp.int32)
    halves = [((zs, own, feat), F32), ((zs, own, feat), BF)]
    keep, give = in_vmem(functools.partial(forward_kernel, own), halves)(here, tile, block)

    chip = keep + swap_core(give).astype(F32)
    sent = chip.astype(BF)
    trio = [[2 * k + c for k in range(zs)] for c in range(2)]
    chips = lax.all_gather(sent, "rep", axis_index_groups=trio).astype(F32)
    totals = chips.sum(axis=0).reshape(half, feat)

    agg_half = (totals * inv_half[:, None]).astype(BF)
    agg_other = swap_core(agg_half)

    lanes = hid // 2
    size = -(-2 * feat // (16 * reps)) * 16
    inner = math.gcd(teams, 8)
    hidden, keep, give, spread = in_vmem(
        functools.partial(middle_kernel, own, size),
        [((own, hid), BF), *halves, ((teams // inner, size, lanes), F32)],
        [((rows, feat), BF), ((rows, hid), BF), ((rows, feat), F32), ((reps * size, lanes), F32)],
    )(here, tile, agg_half, agg_other, cotangent, weight, inv_root[None, :])

    taken = across(give, lambda i, s: (i + 1 if s % 2 == 0 else i - 1, s ^ 1))
    apart = [[b * inner + y for b in range(teams // inner)] for y in range(inner)]
    near = [[b * inner + y for y in range(inner)] for b in range(teams // inner)]

    def sum_over(value, groups):
        return lax.all_to_all(value, "team", 0, 0, axis_index_groups=groups).sum(axis=0)

    def send(value, k):
        return across(value, lambda i, s: (i - s, 2 * ((s // 2 + k) % zs) + s % 2))

    piece = sum_over(spread, apart)
    sent = (keep + taken.astype(F32)).astype(BF)
    piece, sent = lax.optimization_barrier((piece, sent))
    chunks = [lax.dynamic_index_in_dim(sent, (z + k) % zs, 0, keepdims=False) for k in range(zs)]
    spread = jnp.broadcast_to(piece[None], (inner, size, lanes))
    piece = sum_over(spread, near) * (1.0 / math.sqrt(rows * teams))

    high = lax.reduce_precision(piece, 8, 7)
    packed = jnp.concatenate([high.astype(BF), (piece - high).astype(BF)], axis=0)
    stay = send(chunks[0], 0)
    got = [send(jnp.concatenate([chunks[k], packed], axis=0), k) for k in range(1, zs)]
    summed = stay.astype(F32) + sum(g[:own].astype(F32) for g in got)
    grad_features = (summed * inv_own[:, None]).astype(BF)
    pieces = [packed] + [g[own:] for g in got]
    pieces = [p[:size].astype(F32) + p[size:].astype(F32) for p in pieces]
    mine = jnp.stack(
        [jnp.where(z == q, pieces[0], jnp.where(z == (q + 1) % zs, pieces[1], pieces[2])) for q in range(zs)], axis=0
    )
    other = swap_core(mine)
    tall = jnp.stack([jnp.where(core == 0, mine, other), jnp.where(core == 0, other, mine)], axis=1)
    tall = tall.reshape(reps * size, lanes)
    grad_weight = jnp.concatenate([tall[:feat], tall[feat : 2 * feat]], axis=1)
    return (hidden, grad_features, grad_weight)


def solution(mesh):
    in_specs = (
        P("team", None),
        P("team"),
        P("rep", "team", None),
        P("rep", "team"),
        P(),
        P("team", None),
    )
    out_specs = (P(("team", "rep"), None), P(("team", "rep"), None), P())
    return jax.shard_map(local, mesh=mesh, in_specs=in_specs, out_specs=out_specs, check_vma=False)
```

time: 162 us -> 139 us (0.86)
  blocking collectives: 0 us -> 41.4 us
  waiting for transfers between devices: 70 us -> 37 us
  starting transfers between devices: 72.3 us -> 43.2 us
  matrix products: 4.87 us -> 0 us
  Pallas kernels: 0 us -> 4.57 us
  other arithmetic: 7.49 us -> 4.7 us
    all_gather x0 -> x1, blocking collectives: none -> 41.4 us  [local(): chips = lax.all_gather(sent, 'rep', axis_index_groups=trio).astype(F32)]
    ppermute x5 -> x0, starting transfers between devices: 33 us -> none  [the longest x1 23.3 us: local(): lax.ppermute(sent, 'rep', [(s, (s + 2) % reps) for s in range(reps)])]
    ppermute x5 -> x0, waiting for transfers between devices: 27.1 us -> none  [the longest x3 12.3 us: local(): lax.ppermute(piece, 'team', [(i, i ^ bit) for i in range(teams)])]
    all_to_all x2, waiting for transfers between devices: 27.8 us -> 8.43 us  [sum_over(): lax.all_to_all(value, 'team', 0, 0, axis_index_groups=groups).sum(axis=0)]
    ppermute x2 -> x5, starting transfers between devices: 11.5 us -> 29.4 us  [across(): return lax.ppermute(value, ('team', 'rep'), route)]
    all_to_all x2, starting transfers between devices: 23.4 us -> 6.94 us  [sum_over(): lax.all_to_all(value, 'team', 0, 0, axis_index_groups=groups).sum(axis=0)]
    ppermute x2 -> x5, waiting for transfers between devices: 12.9 us -> 25.7 us  [across(): return lax.ppermute(value, ('team', 'rep'), route)]
    dot_general x4 -> x0, matrix products: 4.87 us -> none  [the longest x1 1.92 us: local(): pre_act = jnp.dot(aggregated, weight, preferred_element_type=F32)]
  transfers between devices with their start and end apart: 11 -> 10, of which waited for: 10 -> 7; matrix products, arithmetic and copies ran while one was open for 2% -> 1% of each run, Pallas kernels for 0% -> 0%
where the time goes in v4:
time: 139 us; the launch traced here: 138 us
  starting transfers between devices  43.2 us (31%)
  blocking collectives  41.4 us (30%)
  waiting for transfers between devices  37 us (27%)
  local copies, waits for them, and re-layouts  5.7 us (4%)
  other arithmetic  4.7 us (3%)
  Pallas kernels  4.57 us (3%)
  between operations  1.63 us (1%)
    all_gather x1, blocking collectives, local(): chips = lax.all_gather(sent, 'rep', axis_index_groups=trio).astype(F32)  41.4 us
    ppermute x5, starting transfers between devices, across(): return lax.ppermute(value, ('team', 'rep'), route)  29.4 us
    ppermute x5, waiting for transfers between devices, across(): return lax.ppermute(value, ('team', 'rep'), route)  25.7 us
    all_to_all x2, waiting for transfers between devices, sum_over(): lax.all_to_all(value, 'team', 0, 0, axis_index_groups=groups).sum(axis=0)  8.43 us
    all_to_all x2, starting transfers between devices, sum_over(): lax.all_to_all(value, 'team', 0, 0, axis_index_groups=groups).sum(axis=0)  6.94 us
    ppermute x3, starting transfers between devices, swap_core(): return lax.ppermute(value, 'rep', [(s, s ^ 1) for s in range(reps)])  6.84 us
    unnamed x14, local copies, waits for them, and re-layouts  4.69 us
    pallas_call x2, Pallas kernels, call(): pl.pallas_call(body, out_shape=[jax.ShapeDtypeStruct(shape, dtype) for sh...  4.57 us
  transfers between devices with their start and end apart: 10, of which 7 were waited for; matrix products, arithmetic and copies ran while one was open for 1% of the time, Pallas kernels for 0%

profile of v4, /device:TPU:1, one launch (start us, length us, event | category | flops | bytes accessed | tf_op | source)
XLA Modules:
  0.0 138.2 jit_solution(9346184876478395700)
XLA Ops:
  0.6 0.7 convert_rsqrt_fusion
  1.3 1.2 multiply_convert_fusion
  2.5 4.0 %collective-permute-start = (bf16[1152,128]{1,0:T(8,128)(2,1)S(1)}, bf16[1152,128]{1,0:T(8,128)(2,1)S(1)}, u32[]{:S(2)}, u32[]{:S(2)}) collective-permute-start(bf16[1152,128]{1,0:T(8,128)(2,1)S(1)} %multiply_convert_fusion), channel_id=1, source_target_pairs={{0,0},{1,7},{2,14},{3,21},{4,28},{5,35},{6,6},{7,13},{8,20},{9,27}... | collective-permute-start | bytes 884744 | tf_op jit(solution)/shard_map/ppermute | solution.py:90
  7.2 0.1 pad_add_fusion.here_ref
  7.3 12.9 %collective-permute-done.block_ref = bf16[1152,128]{1,0:T(8,128)(2,1)S(1)} collective-permute-done((bf16[1152,128]{1,0:T(8,128)(2,1)S(1)}, bf16[1152,128]{1,0:T(8,128)(2,1)S(1)}, u32[]{:S(2)}, u32[]{:S(2)}) %collective-permute-start) | collective-permute-done | bytes 294944 | tf_op jit(solution)/shard_map/ppermute | solution.py:90
  20.2 0.0 copy-start
  20.2 1.7 %copy-done = bf16[1,1152,1152]{2,1,0:T(8,128)(2,1)S(1)} copy-done((bf16[1,1152,1152]{2,1,0:T(8,128)(2,1)S(1)}, bf16[1,1152,1152]{2,1,0:T(8,128)(2,1)}, u32[]{:S(2)}) %copy-start) | copy-done | bytes 2654232
  21.9 0.0 copy-start.1
  21.9 0.0 copy-start.2
  21.9 2.0 %shard_map.85 = (f32[3,192,128]{2,1,0:T(8,128)S(1)}, bf16[3,192,128]{2,1,0:T(8,128)(2,1)}) custom-call(s32[3]{0:T(128)S(1)} %pad_add_fusion.here_ref, bf16[1152,1152]{1,0:T(8,128)(2,1)S(1)} %bitcast.28, bf16[1152,128]{1,0:T(8,128)(2,1)S(1)} %collective-permute-done.block_ref), custom_call_target="tpu_custom_call" | custom-call | tf_op jit(solution)/shard_map/pallas_call | solution.py:65
  24.0 0.0 copy-start.4
  24.0 0.7 copy-done.4
  24.7 1.9 %collective-permute-start.1 = (bf16[3,192,128]{2,1,0:T(8,128)(2,1)}, bf16[3,192,128]{2,1,0:T(8,128)(2,1)S(1)}, u32[]{:S(2)}, u32[]{:S(2)}) collective-permute-start(bf16[3,192,128]{2,1,0:T(8,128)(2,1)} %get-tuple-element.12), channel_id=1, source_target_pairs={{0,1},{1,0},{2,3},{3,2},{4,5},{5,4},{6,7},{7,6},{8,9},{9,8},{10,11... | collective-permute-start | bytes 442376 | tf_op jit(solution)/shard_map/ppermute | solution.py:93
  26.6 0.1 reshape.21
  26.7 0.1 mul.37
  26.8 1.4 collective-permute-done.1
  28.1 1.0 add_convert_fusion.1
  29.1 41.4 %all-gather = bf16[9,192,128]{2,1,0:T(8,128)(2,1)S(1)} all-gather(bf16[3,192,128]{2,1,0:T(8,128)(2,1)S(1)} %add_convert_fusion.1), channel_id=2, replica_groups={{0,2,4},{1,3,5},{6,8,10},{7,9,11},{12,14,16},{13,15,17},{18,20,22},{19,..., dimensions={0}, use_global_device_ids=true | all-gather | bytes 589824 | tf_op jit(solution)/shard_map/all_gather | solution.py:112
  70.5 0.1 convert_reduce_fusion
  70.6 0.1 fusion.half_ref
  70.7 3.0 %collective-permute-start.2 = (bf16[576,128]{1,0:T(8,128)(2,1)S(1)}, bf16[576,128]{1,0:T(8,128)(2,1)S(1)}, u32[]{:S(2)}, u32[]{:S(2)}) collective-permute-start(bf16[576,128]{1,0:T(8,128)(2,1)S(1)} %fusion.half_ref), channel_id=1, source_target_pairs={{0,1},{1,0},{2,3},{3,2},{4,5},{5,4},{6,7},{7,6},{8,9},{9,8},{10,11... | collective-permute-start | bytes 442376 | tf_op jit(solution)/shard_map/ppermute | solution.py:93
  73.8 1.0 collective-permute-done.2.other_ref
  74.7 0.0 copy-done.1
  74.8 0.0 copy-done.2
  74.8 0.0 copy-start.5
  74.8 0.8 copy-done.5
  75.6 2.5 %shard_map.86 = (bf16[192,256]{1,0:T(8,128)(2,1)}, f32[3,192,128]{2,1,0:T(8,128)S(1)}, bf16[3,192,128]{2,1,0:T(8,128)(2,1)S(1)}, f32[16,48,128]{2,1,0:T(8,128)S(1)}) custom-call(s32[3]{0:T(128)S(1)} %pad_add_fusion.here_ref, bf16[1152,1152]{1,0:T(8,128)(2,1)S(1)} %bitcast.29, bf16[576,128]{1,0:T(8,128)(2,1)S(1)} %fusion.half_ref, ...), custom_call_target="tpu_custom_call" | custom-call | tf_op jit(solution)/shard_map/pallas_call | solution.py:65
  78.1 0.0 copy-start.3
  78.1 0.7 copy-done.3
  78.9 0.7 copy-done.6
  79.5 3.6 %all-to-all-start = ((f32[16,48,128]{2,1,0:T(8,128)}), f32[16,48,128]{2,1,0:T(8,128)S(1)}, u32[]{:S(2)}, u32[]{:S(2)}) async-start(f32[16,48,128]{2,1,0:T(8,128)} %copy-done.3), calls=%async_computation | async-start | bytes 786432 | tf_op jit(solution)/shard_map/all_to_all | solution.py:132
  83.1 9.4 %collective-permute-start.3 = (bf16[3,192,128]{2,1,0:T(8,128)(2,1)}, bf16[3,192,128]{2,1,0:T(8,128)(2,1)S(1)}, u32[]{:S(2)}, u32[]{:S(2)}) collective-permute-start(bf16[3,192,128]{2,1,0:T(8,128)(2,1)} %copy-done.6), channel_id=1, source_target_pairs={{0,7},{1,762},{2,9},{3,764},{4,11},{5,766},{6,13},{7,0},{8,15},{9,... | collective-permute-start | bytes 442376 | tf_op jit(solution)/shard_map/ppermute | solution.py:90
  92.5 6.6 %collective-permute-done.3 = bf16[3,192,128]{2,1,0:T(8,128)(2,1)S(1)} collective-permute-done((bf16[3,192,128]{2,1,0:T(8,128)(2,1)}, bf16[3,192,128]{2,1,0:T(8,128)(2,1)S(1)}, u32[]{:S(2)}, u32[]{:S(2)}) %collective-permute-start.3) | collective-permute-done | bytes 147488 | tf_op jit(solution)/shard_map/ppermute | solution.py:90
  99.2 0.0 all-to-all-done
  99.2 0.7 broadcast_in_dim.5
  99.9 3.4 %all-to-all-start.1 = ((f32[8,48,128]{2,1,0:T(8,128)}), f32[8,48,128]{2,1,0:T(8,128)S(1)}, u32[]{:S(2)}, u32[]{:S(2)}) async-start(f32[8,48,128]{2,1,0:T(8,128)} %broadcast_in_dim.5), calls=%async_computation.1 | async-start | bytes 393216 | tf_op jit(solution)/shard_map/all_to_all | solution.py:132
  103.4 8.4 %all-to-all-done.1 = f32[8,48,128]{2,1,0:T(8,128)S(1)} async-done(((f32[8,48,128]{2,1,0:T(8,128)}), f32[8,48,128]{2,1,0:T(8,128)S(1)}, u32[]{:S(2)}, u32[]{:S(2)}) %all-to-all-start.1) | async-done | bytes 196640 | tf_op jit(solution)/shard_map/all_to_all | solution.py:132
  111.9 5.2 %collective-permute-start.5 = (bf16[288,128]{1,0:T(8,128)(2,1)S(1)}, bf16[288,128]{1,0:T(8,128)(2,1)S(1)}, u32[]{:S(2)}, u32[]{:S(2)}) collective-permute-start(bf16[288,128]{1,0:T(8,128)(2,1)S(1)} %get-tuple-element.29), channel_id=1, source_target_pairs={{0,2},{1,765},{2,760},{3,755},{4,744},{5,739},{6,8},{7,3},{8,766},... | collective-permute-start | bytes 221192 | tf_op jit(solution)/shard_map/ppermute | solution.py:90
  117.1 4.3 %collective-permute-start.6 = (bf16[288,128]{1,0:T(8,128)(2,1)S(1)}, bf16[288,128]{1,0:T(8,128)(2,1)S(1)}, u32[]{:S(2)}, u32[]{:S(2)}) collective-permute-start(bf16[288,128]{1,0:T(8,128)(2,1)S(1)} %get-tuple-element.30), channel_id=1, source_target_pairs={{0,4},{1,767},{2,756},{3,751},{4,746},{5,741},{6,10},{7,5},{8,762}... | collective-permute-start | bytes 221192 | tf_op jit(solution)/shard_map/ppermute | solution.py:90
  121.4 0.1 dynamic_slice.21
  121.5 6.5 %collective-permute-start.4 = (bf16[192,128]{1,0:T(8,128)(2,1)S(1)}, bf16[192,128]{1,0:T(8,128)(2,1)S(1)}, u32[]{:S(2)}, u32[]{:S(2)}) collective-permute-start(bf16[192,128]{1,0:T(8,128)(2,1)S(1)} %get-tuple-element.28), channel_id=1, source_target_pairs={{0,0},{1,763},{2,758},{3,753},{4,748},{5,743},{6,6},{7,1},{8,764},... | collective-permute-start | bytes 147464 | tf_op jit(solution)/shard_map/ppermute | solution.py:90
  128.0 0.0 collective-permute-done.5
  128.0 6.2 %collective-permute-done.6 = bf16[288,128]{1,0:T(8,128)(2,1)S(1)} collective-permute-done((bf16[288,128]{1,0:T(8,128)(2,1)S(1)}, bf16[288,128]{1,0:T(8,128)(2,1)S(1)}, u32[]{:S(2)}, u32[]{:S(2)}) %collective-permute-start.6) | collective-permute-done | bytes 73760 | tf_op jit(solution)/shard_map/ppermute | solution.py:90
  134.3 1.9 %collective-permute-start.7 = (f32[3,48,128]{2,1,0:T(8,128)S(1)}, f32[3,48,128]{2,1,0:T(8,128)S(1)}, u32[]{:S(2)}, u32[]{:S(2)}) collective-permute-start(f32[3,48,128]{2,1,0:T(8,128)S(1)} %pad_maximum_fusion.6), channel_id=1, source_target_pairs={{0,1},{1,0},{2,3},{3,2},{4,5},{5,4},{6,7},{7,6},{8,9},{9,8},{10,11... | collective-permute-start | bytes 221192 | tf_op jit(solution)/shard_map/ppermute | solution.py:93
  136.2 0.0 collective-permute-done.4
  136.2 0.7 multiply_convert_fusion.1
  136.9 0.5 collective-permute-done.7
  137.5 0.7 pad_maximum_fusion.1
  (15 shorter events, 0.2 us)
Async XLA Ops:
  2.5 17.7 %collective-permute-start = (bf16[1152,128]{1,0:T(8,128)(2,1)S(1)}, bf16[1152,128]{1,0:T(8,128)(2,1)S(1)}, u32[]{:S(2)}, u32[]{:S(2)}) collective-permute-start(bf16[1152,128]{1,0:T(8,128)(2,1)S(1)} %multiply_convert_fusion), channel_id=1, source_target_pairs={{0,0},{1,7},{2,14},{3,21},{4,28},{5,35},{6,6},{7,13},{8,20},{9,27}... | collective-permute-start | bytes 884744 | tf_op jit(solution)/shard_map/ppermute | solution.py:90
  20.2 1.8 %copy-start = (bf16[1,1152,1152]{2,1,0:T(8,128)(2,1)S(1)}, bf16[1,1152,1152]{2,1,0:T(8,128)(2,1)}, u32[]{:S(2)}) copy-start(bf16[1,1152,1152]{2,1,0:T(8,128)(2,1)} %param.8) | copy-start | bytes 7962628
  21.9 52.8 %copy-start.1 = (bf16[1,1152,1152]{2,1,0:T(8,128)(2,1)S(1)}, bf16[1,1152,1152]{2,1,0:T(8,128)(2,1)}, u32[]{:S(2)}) copy-start(bf16[1,1152,1152]{2,1,0:T(8,128)(2,1)} %param.8) | copy-start | bytes 7962628
  21.9 52.8 %copy-start.2 = (bf16[1152,256]{1,0:T(8,128)(2,1)S(1)}, bf16[1152,256]{1,0:T(8,128)(2,1)}, u32[]{:S(2)}) copy-start(bf16[1152,256]{1,0:T(8,128)(2,1)} %cot_ref.1) | copy-start | bytes 1769476
  24.0 0.7 copy-start.4
  24.7 3.5 %collective-permute-start.1 = (bf16[3,192,128]{2,1,0:T(8,128)(2,1)}, bf16[3,192,128]{2,1,0:T(8,128)(2,1)S(1)}, u32[]{:S(2)}, u32[]{:S(2)}) collective-permute-start(bf16[3,192,128]{2,1,0:T(8,128)(2,1)} %get-tuple-element.12), channel_id=1, source_target_pairs={{0,1},{1,0},{2,3},{3,2},{4,5},{5,4},{6,7},{7,6},{8,9},{9,8},{10,11... | collective-permute-start | bytes 442376 | tf_op jit(solution)/shard_map/ppermute | solution.py:93
  70.7 4.0 %collective-permute-start.2 = (bf16[576,128]{1,0:T(8,128)(2,1)S(1)}, bf16[576,128]{1,0:T(8,128)(2,1)S(1)}, u32[]{:S(2)}, u32[]{:S(2)}) collective-permute-start(bf16[576,128]{1,0:T(8,128)(2,1)S(1)} %fusion.half_ref), channel_id=1, source_target_pairs={{0,1},{1,0},{2,3},{3,2},{4,5},{5,4},{6,7},{7,6},{8,9},{9,8},{10,11... | collective-permute-start | bytes 442376 | tf_op jit(solution)/shard_map/ppermute | solution.py:93
  74.8 0.8 copy-start.5
  78.1 0.7 copy-start.3
  78.9 0.7 copy-start.6
  79.5 19.6 %all-to-all-start = ((f32[16,48,128]{2,1,0:T(8,128)}), f32[16,48,128]{2,1,0:T(8,128)S(1)}, u32[]{:S(2)}, u32[]{:S(2)}) async-start(f32[16,48,128]{2,1,0:T(8,128)} %copy-done.3), calls=%async_computation | async-start | bytes 786432 | tf_op jit(solution)/shard_map/all_to_all | solution.py:132
  83.1 16.0 %collective-permute-start.3 = (bf16[3,192,128]{2,1,0:T(8,128)(2,1)}, bf16[3,192,128]{2,1,0:T(8,128)(2,1)S(1)}, u32[]{:S(2)}, u32[]{:S(2)}) collective-permute-start(bf16[3,192,128]{2,1,0:T(8,128)(2,1)} %copy-done.6), channel_id=1, source_target_pairs={{0,7},{1,762},{2,9},{3,764},{4,11},{5,766},{6,13},{7,0},{8,15},{9,... | collective-permute-start | bytes 442376 | tf_op jit(solution)/shard_map/ppermute | solution.py:90
  99.9 11.9 %all-to-all-start.1 = ((f32[8,48,128]{2,1,0:T(8,128)}), f32[8,48,128]{2,1,0:T(8,128)S(1)}, u32[]{:S(2)}, u32[]{:S(2)}) async-start(f32[8,48,128]{2,1,0:T(8,128)} %broadcast_in_dim.5), calls=%async_computation.1 | async-start | bytes 393216 | tf_op jit(solution)/shard_map/all_to_all | solution.py:132
  111.9 16.1 %collective-permute-start.5 = (bf16[288,128]{1,0:T(8,128)(2,1)S(1)}, bf16[288,128]{1,0:T(8,128)(2,1)S(1)}, u32[]{:S(2)}, u32[]{:S(2)}) collective-permute-start(bf16[288,128]{1,0:T(8,128)(2,1)S(1)} %get-tuple-element.29), channel_id=1, source_target_pairs={{0,2},{1,765},{2,760},{3,755},{4,744},{5,739},{6,8},{7,3},{8,766},... | collective-permute-start | bytes 221192 | tf_op jit(solution)/shard_map/ppermute | solution.py:90
  117.1 17.1 %collective-permute-start.6 = (bf16[288,128]{1,0:T(8,128)(2,1)S(1)}, bf16[288,128]{1,0:T(8,128)(2,1)S(1)}, u32[]{:S(2)}, u32[]{:S(2)}) collective-permute-start(bf16[288,128]{1,0:T(8,128)(2,1)S(1)} %get-tuple-element.30), channel_id=1, source_target_pairs={{0,4},{1,767},{2,756},{3,751},{4,746},{5,741},{6,10},{7,5},{8,762}... | collective-permute-start | bytes 221192 | tf_op jit(solution)/shard_map/ppermute | solution.py:90
  121.5 14.7 %collective-permute-start.4 = (bf16[192,128]{1,0:T(8,128)(2,1)S(1)}, bf16[192,128]{1,0:T(8,128)(2,1)S(1)}, u32[]{:S(2)}, u32[]{:S(2)}) collective-permute-start(bf16[192,128]{1,0:T(8,128)(2,1)S(1)} %get-tuple-element.28), channel_id=1, source_target_pairs={{0,0},{1,763},{2,758},{3,753},{4,748},{5,743},{6,6},{7,1},{8,764},... | collective-permute-start | bytes 147464 | tf_op jit(solution)/shard_map/ppermute | solution.py:90
  134.3 3.2 %collective-permute-start.7 = (f32[3,48,128]{2,1,0:T(8,128)S(1)}, f32[3,48,128]{2,1,0:T(8,128)S(1)}, u32[]{:S(2)}, u32[]{:S(2)}) collective-permute-start(f32[3,48,128]{2,1,0:T(8,128)S(1)} %pad_maximum_fusion.6), channel_id=1, source_target_pairs={{0,1},{1,0},{2,3},{3,2},{4,5},{5,4},{6,7},{7,6},{8,9},{9,8},{10,11... | collective-permute-start | bytes 221192 | tf_op jit(solution)/shard_map/ppermute | solution.py:93

commit v5 on v4

--- a/solution.py
+++ b/solution.py
@@ -12,20 +12,20 @@
 F32 = jnp.float32
 
 
-def forward_kernel(own, here_ref, tile_ref, block_ref, keep_ref, give_ref):
+def split_kernel(own, here_ref, term_ref, keep_ref, give_ref, rows_ref):
     core, tile_on = here_ref[0], here_ref[2].astype(F32)
+    rows_ref[...] = (term_ref[...] * tile_on).T
     for q in range(keep_ref.shape[0]):
         for out_ref, side in ((keep_ref, core), (give_ref, 1 - core)):
             start = pl.multiple_of((2 * q + side) * own, own)
-            term = jnp.dot(tile_ref[pl.ds(start, own), :], block_ref[...], preferred_element_type=F32)
-            out_ref[q] = (term * tile_on).astype(out_ref.dtype)
+            out_ref[q] = rows_ref[pl.ds(start, own), :].astype(out_ref.dtype)
 
 
 def middle_kernel(
-    own, size, here_ref, tile_ref, half_ref, other_ref, cot_ref, weight_ref, inv_ref,
-    hidden_ref, keep_ref, give_ref, spread_ref, agg, slope, back, tall,
+    own, size, here_ref, half_ref, other_ref, cot_ref, weight_ref, inv_ref,
+    hidden_ref, message_ref, spread_ref, agg, slope, tall,
 ):
-    core, rep, tile_on = here_ref[0], here_ref[1], here_ref[2].astype(F32)
+    core, rep = here_ref[0], here_ref[1]
     rows, feat = agg.shape
     lanes = tall.shape[1]
     zs = rows // (2 * own)
@@ -43,12 +43,7 @@
         slope[q * own : (q + 1) * own, :] = term
         grad = grad + lax.dot_general(part, term, (((0,), (0,)), ((), ())), preferred_element_type=F32)
     message = lax.dot_general(weight, slope[...], (((1,), (1,)), ((), ())), preferred_element_type=F32)
-    message = (message * inv_ref[...]).astype(BF)
-    back[...] = (jnp.dot(message, tile_ref[...], preferred_element_type=F32) * tile_on).T
-    for q in range(zs):
-        for out_ref, side in ((keep_ref, core), (give_ref, 1 - core)):
-            start = pl.multiple_of((2 * q + side) * own, own)
-            out_ref[q] = back[pl.ds(start, own), :].astype(out_ref.dtype)
+    message_ref[...] = (message * inv_ref[...]).astype(BF)
     tall[:feat, :] = grad[:, :lanes]
     tall[feat : 2 * feat, :] = grad[:, lanes:]
     tall[2 * feat :, :] = jnp.zeros((tall.shape[0] - 2 * feat, lanes), F32)
@@ -92,19 +87,21 @@
     def swap_core(value):
         return lax.ppermute(value, "rep", [(s, s ^ 1) for s in range(reps)])
 
-    def pick(array, which):
-        return lax.dynamic_index_in_dim(array, which, 1, keepdims=False)
+    inv_root = 1.0 / jnp.sqrt(degrees.astype(F32))
 
-    inv_root = 1.0 / jnp.sqrt(degrees.astype(F32))
-    inv_half = pick(inv_root.reshape(zs, 2, own), core).reshape(half)
-    inv_own = lax.dynamic_slice_in_dim(inv_root, rep * own, own, 0)
+    def inv_rows(chunk):
+        return jnp.broadcast_to(lax.dynamic_slice_in_dim(inv_root, chunk * own, own, 0)[:, None], (own, feat))
+
+    inv_half, inv_own = jnp.concatenate([inv_rows(2 * q + core) for q in range(zs)], axis=0), inv_rows(rep)
     source = (features.astype(F32) * inv_root[:, None]).astype(BF)
     tile = tiles[0]
 
     block = across(source, lambda i, s: (i + s, s))
+    block, inv_half, inv_own = lax.optimization_barrier((block, inv_half, inv_own))
     here = jnp.stack([core, rep, pattern[0, 0]]).astype(jnp.int32)
     halves = [((zs, own, feat), F32), ((zs, own, feat), BF)]
-    keep, give = in_vmem(functools.partial(forward_kernel, own), halves)(here, tile, block)
+    split = in_vmem(functools.partial(split_kernel, own), halves, [((rows, feat), F32)])
+    keep, give = split(here, lax.dot_general(block, tile, (((0,), (1,)), ((), ())), preferred_element_type=F32))
 
     chip = keep + swap_core(give).astype(F32)
     sent = chip.astype(BF)
@@ -112,17 +109,18 @@
     chips = lax.all_gather(sent, "rep", axis_index_groups=trio).astype(F32)
     totals = chips.sum(axis=0).reshape(half, feat)
 
-    agg_half = (totals * inv_half[:, None]).astype(BF)
+    agg_half = (totals * inv_half).astype(BF)
     agg_other = swap_core(agg_half)
 
     lanes = hid // 2
     size = -(-2 * feat // (16 * reps)) * 16
     inner = math.gcd(teams, 8)
-    hidden, keep, give, spread = in_vmem(
+    hidden, message, spread = in_vmem(
         functools.partial(middle_kernel, own, size),
-        [((own, hid), BF), *halves, ((teams // inner, size, lanes), F32)],
-        [((rows, feat), BF), ((rows, hid), BF), ((rows, feat), F32), ((reps * size, lanes), F32)],
-    )(here, tile, agg_half, agg_other, cotangent, weight, inv_root[None, :])
+        [((own, hid), BF), ((feat, rows), BF), ((teams // inner, size, lanes), F32)],
+        [((rows, feat), BF), ((rows, hid), BF), ((reps * size, lanes), F32)],
+    )(here, agg_half, agg_other, cotangent, weight, inv_root[None, :])
+    keep, give = split(here, jnp.dot(message, tile, preferred_element_type=F32))
 
     taken = across(give, lambda i, s: (i + 1 if s % 2 == 0 else i - 1, s ^ 1))
     apart = [[b * inner + y for b in range(teams // inner)] for y in range(inner)]
@@ -146,7 +144,7 @@
     stay = send(chunks[0], 0)
     got = [send(jnp.concatenate([chunks[k], packed], axis=0), k) for k in range(1, zs)]
     summed = stay.astype(F32) + sum(g[:own].astype(F32) for g in got)
-    grad_features = (summed * inv_own[:, None]).astype(BF)
+    grad_features = (summed * inv_own).astype(BF)
     pieces = [packed] + [g[own:] for g in got]
     pieces = [p[:size].astype(F32) + p[size:].astype(F32) for p in pieces]
     mine = jnp.stack(

time: 139 us -> 132 us (0.950)
  waiting for transfers between devices: 37 us -> 31.2 us
  local copies, waits for them, and re-layouts: 5.7 us -> 1.71 us
  starting transfers between devices: 43.2 us -> 46.5 us
  matrix products: 0 us -> 1.52 us
    ppermute x5, waiting for transfers between devices: 25.7 us -> 20.3 us  [across(): return lax.ppermute(value, ('team', 'rep'), route)]
    unnamed x14 -> x8, local copies, waits for them, and re-layouts: 4.69 us -> 0.03 us
    ppermute x3, starting transfers between devices: 6.84 us -> 10.3 us  [swap_core(): return lax.ppermute(value, 'rep', [(s, s ^ 1) for s in range(reps)])]
    dot_general x0 -> x2, matrix products: none -> 1.52 us  [the longest x1 0.94 us: local(): lax.dot_general(block, tile, (((0,), (1,)), ((), ())), preferred_element_...]
    pallas_call x2 -> x3, Pallas kernels: 4.57 us -> 3.71 us  [call(): pl.pallas_call(body, out_shape=[jax.ShapeDtypeStruct(shape, dtype) for sh...]
  transfers between devices with their start and end apart: 10 -> 10, of which waited for: 7 -> 7; matrix products, arithmetic and copies ran while one was open for 1% -> 1% of each run, Pallas kernels for 0% -> 1%
where the time goes in v5:
time: 132 us
  starting transfers between devices  46.5 us (35%)
  blocking collectives  41.4 us (31%)
  waiting for transfers between devices  31.2 us (24%)
  other arithmetic  3.81 us (3%)
  Pallas kernels  3.71 us (3%)
  local copies, waits for them, and re-layouts  1.71 us (1%)
  between operations  1.7 us (1%)
  matrix products  1.52 us (1%)
    all_gather x1, blocking collectives, local(): chips = lax.all_gather(sent, 'rep', axis_index_groups=trio).astype(F32)  41.4 us
    ppermute x5, starting transfers between devices, across(): return lax.ppermute(value, ('team', 'rep'), route)  29.2 us
    ppermute x5, waiting for transfers between devices, across(): return lax.ppermute(value, ('team', 'rep'), route)  20.3 us
    ppermute x3, starting transfers between devices, swap_core(): return lax.ppermute(value, 'rep', [(s, s ^ 1) for s in range(reps)])  10.3 us
    all_to_all x2, waiting for transfers between devices, sum_over(): lax.all_to_all(value, 'team', 0, 0, axis_index_groups=groups).sum(axis=0)  8.44 us
    all_to_all x2, starting transfers between devices, sum_over(): lax.all_to_all(value, 'team', 0, 0, axis_index_groups=groups).sum(axis=0)  6.94 us
    pallas_call x3, Pallas kernels, call(): pl.pallas_call(body, out_shape=[jax.ShapeDtypeStruct(shape, dtype) for sh...  3.71 us
  transfers between devices with their start and end apart: 10, of which 7 were waited for; matrix products, arithmetic and copies ran while one was open for 1% of the time, Pallas kernels for 1%

profile of v5, /device:TPU:1, one launch (start us, length us, event | category | flops | bytes accessed | tf_op | source)
XLA Modules:
  0.0 131.6 jit_solution(6182203583021690675)
XLA Ops:
  0.6 0.0 copy-start
  0.6 0.9 convert_rsqrt_fusion
  1.5 1.2 multiply_convert_fusion
  2.7 4.0 %collective-permute-start = (bf16[1152,128]{1,0:T(8,128)(2,1)S(1)}, bf16[1152,128]{1,0:T(8,128)(2,1)S(1)}, u32[]{:S(2)}, u32[]{:S(2)}) collective-permute-start(bf16[1152,128]{1,0:T(8,128)(2,1)S(1)} %multiply_convert_fusion), channel_id=1, source_target_pairs={{0,0},{1,7},{2,14},{3,21},{4,28},{5,35},{6,6},{7,13},{8,20},{9,27}... | collective-permute-start | bytes 884744 | tf_op jit(solution)/shard_map/ppermute | solution.py:85
  7.4 0.1 pad_add_fusion.here_ref
  7.5 0.1 fusion.7
  7.6 0.1 maximum_maximum_fusion
  7.7 12.7 %collective-permute-done = bf16[1152,128]{1,0:T(8,128)(2,1)S(1)} collective-permute-done((bf16[1152,128]{1,0:T(8,128)(2,1)S(1)}, bf16[1152,128]{1,0:T(8,128)(2,1)S(1)}, u32[]{:S(2)}, u32[]{:S(2)}) %collective-permute-start) | collective-permute-done | bytes 294944 | tf_op jit(solution)/shard_map/ppermute | solution.py:85
  20.3 0.7 broadcast_in_dim.15
  21.1 0.1 broadcast.12
  21.2 0.0 copy-done
  21.2 0.0 copy-start.1
  21.2 0.0 copy-start.2
  21.2 0.9 fusion.2.term_ref
  22.2 0.8 shard_map.85
  23.0 1.9 %collective-permute-start.1 = (bf16[3,192,128]{2,1,0:T(8,128)(2,1)S(1)}, bf16[3,192,128]{2,1,0:T(8,128)(2,1)S(1)}, u32[]{:S(2)}, u32[]{:S(2)}) collective-permute-start(bf16[3,192,128]{2,1,0:T(8,128)(2,1)S(1)} %get-tuple-element.17), channel_id=1, source_target_pairs={{0,1},{1,0},{2,3},{3,2},{4,5},{5,4},{6,7},{7,6},{8,9},{9,8},{10,11... | collective-permute-start | bytes 442376 | tf_op jit(solution)/shard_map/ppermute | solution.py:88
  24.9 1.3 %collective-permute-done.1 = bf16[3,192,128]{2,1,0:T(8,128)(2,1)S(1)} collective-permute-done((bf16[3,192,128]{2,1,0:T(8,128)(2,1)S(1)}, bf16[3,192,128]{2,1,0:T(8,128)(2,1)S(1)}, u32[]{:S(2)}, u32[]{:S(2)}) %collective-permute-start.1) | collective-permute-done | bytes 147488 | tf_op jit(solution)/shard_map/ppermute | solution.py:88
  26.3 41.4 %all-gather = bf16[9,192,128]{2,1,0:T(8,128)(2,1)S(1)} all-gather(bf16[3,192,128]{2,1,0:T(8,128)(2,1)S(1)} %add_convert_fusion.1), channel_id=2, replica_groups={{0,2,4},{1,3,5},{6,8,10},{7,9,11},{12,14,16},{13,15,17},{18,20,22},{19,..., dimensions={0}, use_global_device_ids=true | all-gather | bytes 589824 | tf_op jit(solution)/shard_map/all_gather | solution.py:109
  67.7 0.1 convert_reduce_fusion
  67.8 3.0 %collective-permute-start.2 = (bf16[576,128]{1,0:T(8,128)(2,1)S(1)}, bf16[576,128]{1,0:T(8,128)(2,1)S(1)}, u32[]{:S(2)}, u32[]{:S(2)}) collective-permute-start(bf16[576,128]{1,0:T(8,128)(2,1)S(1)} %fusion.4.half_ref), channel_id=1, source_target_pairs={{0,1},{1,0},{2,3},{3,2},{4,5},{5,4},{6,7},{7,6},{8,9},{9,8},{10,11... | collective-permute-start | bytes 442376 | tf_op jit(solution)/shard_map/ppermute | solution.py:88
  70.9 1.0 collective-permute-done.2.other_ref
  71.8 0.0 copy-done.1
  71.8 0.0 copy-done.2
  71.8 2.1 %shard_map.86 = (bf16[192,256]{1,0:T(8,128)(2,1)}, bf16[128,1152]{1,0:T(8,128)(2,1)S(1)}, f32[16,48,128]{2,1,0:T(8,128)}) custom-call(s32[3]{0:T(128)S(1)} %pad_add_fusion.here_ref, bf16[576,128]{1,0:T(8,128)(2,1)S(1)} %fusion.4.half_ref, bf16[576,128]{1,0:T(8,128)(2,1)S(1)} %collective-permute-done.2.other_ref, bf16[1152,256]{1,0:T(8,128)(2,1)S(1)} %copy-done.1, ...), custom_call_target="tpu_custom_call" | custom-call | tf_op jit(solution)/shard_map/pallas_call | solution.py:60
  73.9 3.6 %all-to-all-start = ((f32[16,48,128]{2,1,0:T(8,128)}), f32[16,48,128]{2,1,0:T(8,128)S(1)}, u32[]{:S(2)}, u32[]{:S(2)}) async-start(f32[16,48,128]{2,1,0:T(8,128)} %get-tuple-element.20), calls=%async_computation | async-start | bytes 786432 | tf_op jit(solution)/shard_map/all_to_all | solution.py:130
  77.5 0.6 fusion.term_ref
  78.1 0.0 copy-start.3
  78.1 0.8 shard_map.87
  78.9 9.4 %collective-permute-start.3 = (bf16[3,192,128]{2,1,0:T(8,128)(2,1)S(1)}, bf16[3,192,128]{2,1,0:T(8,128)(2,1)S(1)}, u32[]{:S(2)}, u32[]{:S(2)}) collective-permute-start(bf16[3,192,128]{2,1,0:T(8,128)(2,1)S(1)} %get-tuple-element.23), channel_id=1, source_target_pairs={{0,7},{1,762},{2,9},{3,764},{4,11},{5,766},{6,13},{7,0},{8,15},{9,... | collective-permute-start | bytes 442376 | tf_op jit(solution)/shard_map/ppermute | solution.py:85
  88.3 5.2 %collective-permute-done.3 = bf16[3,192,128]{2,1,0:T(8,128)(2,1)S(1)} collective-permute-done((bf16[3,192,128]{2,1,0:T(8,128)(2,1)S(1)}, bf16[3,192,128]{2,1,0:T(8,128)(2,1)S(1)}, u32[]{:S(2)}, u32[]{:S(2)}) %collective-permute-start.3) | collective-permute-done | bytes 147488 | tf_op jit(solution)/shard_map/ppermute | solution.py:85
  93.5 0.0 all-to-all-done
  93.6 0.7 broadcast_in_dim.17
  94.3 3.4 %all-to-all-start.1 = ((f32[8,48,128]{2,1,0:T(8,128)}), f32[8,48,128]{2,1,0:T(8,128)S(1)}, u32[]{:S(2)}, u32[]{:S(2)}) async-start(f32[8,48,128]{2,1,0:T(8,128)} %broadcast_in_dim.17), calls=%async_computation.1 | async-start | bytes 393216 | tf_op jit(solution)/shard_map/all_to_all | solution.py:130
  97.8 8.4 %all-to-all-done.1 = f32[8,48,128]{2,1,0:T(8,128)S(1)} async-done(((f32[8,48,128]{2,1,0:T(8,128)}), f32[8,48,128]{2,1,0:T(8,128)S(1)}, u32[]{:S(2)}, u32[]{:S(2)}) %all-to-all-start.1) | async-done | bytes 196640 | tf_op jit(solution)/shard_map/all_to_all | solution.py:130
  106.3 5.2 %collective-permute-start.5 = (bf16[288,128]{1,0:T(8,128)(2,1)S(1)}, bf16[288,128]{1,0:T(8,128)(2,1)S(1)}, u32[]{:S(2)}, u32[]{:S(2)}) collective-permute-start(bf16[288,128]{1,0:T(8,128)(2,1)S(1)} %get-tuple-element.37), channel_id=1, source_target_pairs={{0,2},{1,765},{2,760},{3,755},{4,744},{5,739},{6,8},{7,3},{8,766},... | collective-permute-start | bytes 221192 | tf_op jit(solution)/shard_map/ppermute | solution.py:85
  111.5 4.3 %collective-permute-start.6 = (bf16[288,128]{1,0:T(8,128)(2,1)S(1)}, bf16[288,128]{1,0:T(8,128)(2,1)S(1)}, u32[]{:S(2)}, u32[]{:S(2)}) collective-permute-start(bf16[288,128]{1,0:T(8,128)(2,1)S(1)} %get-tuple-element.38), channel_id=1, source_target_pairs={{0,4},{1,767},{2,756},{3,751},{4,746},{5,741},{6,10},{7,5},{8,762}... | collective-permute-start | bytes 221192 | tf_op jit(solution)/shard_map/ppermute | solution.py:85
  115.8 6.3 %collective-permute-start.4 = (bf16[192,128]{1,0:T(8,128)(2,1)S(1)}, bf16[192,128]{1,0:T(8,128)(2,1)S(1)}, u32[]{:S(2)}, u32[]{:S(2)}) collective-permute-start(bf16[192,128]{1,0:T(8,128)(2,1)S(1)} %get-tuple-element.36), channel_id=1, source_target_pairs={{0,0},{1,763},{2,758},{3,753},{4,748},{5,743},{6,6},{7,1},{8,764},... | collective-permute-start | bytes 147464 | tf_op jit(solution)/shard_map/ppermute | solution.py:85
  122.1 0.0 collective-permute-done.5
  122.1 2.4 %collective-permute-done.6 = bf16[288,128]{1,0:T(8,128)(2,1)S(1)} collective-permute-done((bf16[288,128]{1,0:T(8,128)(2,1)S(1)}, bf16[288,128]{1,0:T(8,128)(2,1)S(1)}, u32[]{:S(2)}, u32[]{:S(2)}) %collective-permute-start.6) | collective-permute-done | bytes 73760 | tf_op jit(solution)/shard_map/ppermute | solution.py:85
  124.5 5.4 %collective-permute-start.7 = (f32[3,48,128]{2,1,0:T(8,128)S(1)}, f32[3,48,128]{2,1,0:T(8,128)S(1)}, u32[]{:S(2)}, u32[]{:S(2)}) collective-permute-start(f32[3,48,128]{2,1,0:T(8,128)S(1)} %pad_maximum_fusion.6), channel_id=1, source_target_pairs={{0,1},{1,0},{2,3},{3,2},{4,5},{5,4},{6,7},{7,6},{8,9},{9,8},{10,11... | collective-permute-start | bytes 221192 | tf_op jit(solution)/shard_map/ppermute | solution.py:88
  129.9 0.0 collective-permute-done.4
  129.9 0.0 copy-done.3
  129.9 0.6 multiply_convert_fusion.1
  130.6 0.2 collective-permute-done.7
  130.9 0.7 pad_maximum_fusion.1
  (15 shorter events, 0.3 us)
Async XLA Ops:
  0.6 20.6 %copy-start = (bf16[1,1152,1152]{2,1,0:T(8,128)(2,1)S(1)}, bf16[1,1152,1152]{2,1,0:T(8,128)(2,1)}, u32[]{:S(2)}) copy-start(bf16[1,1152,1152]{2,1,0:T(8,128)(2,1)} %param.8) | copy-start | bytes 7962628
  2.7 17.7 %collective-permute-start = (bf16[1152,128]{1,0:T(8,128)(2,1)S(1)}, bf16[1152,128]{1,0:T(8,128)(2,1)S(1)}, u32[]{:S(2)}, u32[]{:S(2)}) collective-permute-start(bf16[1152,128]{1,0:T(8,128)(2,1)S(1)} %multiply_convert_fusion), channel_id=1, source_target_pairs={{0,0},{1,7},{2,14},{3,21},{4,28},{5,35},{6,6},{7,13},{8,20},{9,27}... | collective-permute-start | bytes 884744 | tf_op jit(solution)/shard_map/ppermute | solution.py:85
  21.2 50.6 %copy-start.1 = (bf16[1152,256]{1,0:T(8,128)(2,1)S(1)}, bf16[1152,256]{1,0:T(8,128)(2,1)}, u32[]{:S(2)}) copy-start(bf16[1152,256]{1,0:T(8,128)(2,1)} %cot_ref.1) | copy-start | bytes 1769476
  21.2 50.6 %copy-start.2 = (bf16[128,256]{1,0:T(8,128)(2,1)S(1)}, bf16[128,256]{1,0:T(8,128)(2,1)}, u32[]{:S(2)}) copy-start(bf16[128,256]{1,0:T(8,128)(2,1)} %weight_ref.1) | copy-start | bytes 196612
  23.0 3.3 %collective-permute-start.1 = (bf16[3,192,128]{2,1,0:T(8,128)(2,1)S(1)}, bf16[3,192,128]{2,1,0:T(8,128)(2,1)S(1)}, u32[]{:S(2)}, u32[]{:S(2)}) collective-permute-start(bf16[3,192,128]{2,1,0:T(8,128)(2,1)S(1)} %get-tuple-element.17), channel_id=1, source_target_pairs={{0,1},{1,0},{2,3},{3,2},{4,5},{5,4},{6,7},{7,6},{8,9},{9,8},{10,11... | collective-permute-start | bytes 442376 | tf_op jit(solution)/shard_map/ppermute | solution.py:88
  67.8 4.0 %collective-permute-start.2 = (bf16[576,128]{1,0:T(8,128)(2,1)S(1)}, bf16[576,128]{1,0:T(8,128)(2,1)S(1)}, u32[]{:S(2)}, u32[]{:S(2)}) collective-permute-start(bf16[576,128]{1,0:T(8,128)(2,1)S(1)} %fusion.4.half_ref), channel_id=1, source_target_pairs={{0,1},{1,0},{2,3},{3,2},{4,5},{5,4},{6,7},{7,6},{8,9},{9,8},{10,11... | collective-permute-start | bytes 442376 | tf_op jit(solution)/shard_map/ppermute | solution.py:88
  73.9 19.6 %all-to-all-start = ((f32[16,48,128]{2,1,0:T(8,128)}), f32[16,48,128]{2,1,0:T(8,128)S(1)}, u32[]{:S(2)}, u32[]{:S(2)}) async-start(f32[16,48,128]{2,1,0:T(8,128)} %get-tuple-element.20), calls=%async_computation | async-start | bytes 786432 | tf_op jit(solution)/shard_map/all_to_all | solution.py:130
  78.1 51.9 %copy-start.3 = (f32[192,128]{1,0:T(8,128)S(1)}, f32[192,128]{1,0:T(8,128)}, u32[]{:S(2)}) copy-start(f32[192,128]{1,0:T(8,128)} %broadcast_in_dim.15) | copy-start | bytes 294916
  78.9 14.6 %collective-permute-start.3 = (bf16[3,192,128]{2,1,0:T(8,128)(2,1)S(1)}, bf16[3,192,128]{2,1,0:T(8,128)(2,1)S(1)}, u32[]{:S(2)}, u32[]{:S(2)}) collective-permute-start(bf16[3,192,128]{2,1,0:T(8,128)(2,1)S(1)} %get-tuple-element.23), channel_id=1, source_target_pairs={{0,7},{1,762},{2,9},{3,764},{4,11},{5,766},{6,13},{7,0},{8,15},{9,... | collective-permute-start | bytes 442376 | tf_op jit(solution)/shard_map/ppermute | solution.py:85
  94.3 11.9 %all-to-all-start.1 = ((f32[8,48,128]{2,1,0:T(8,128)}), f32[8,48,128]{2,1,0:T(8,128)S(1)}, u32[]{:S(2)}, u32[]{:S(2)}) async-start(f32[8,48,128]{2,1,0:T(8,128)} %broadcast_in_dim.17), calls=%async_computation.1 | async-start | bytes 393216 | tf_op jit(solution)/shard_map/all_to_all | solution.py:130
  106.3 15.8 %collective-permute-start.5 = (bf16[288,128]{1,0:T(8,128)(2,1)S(1)}, bf16[288,128]{1,0:T(8,128)(2,1)S(1)}, u32[]{:S(2)}, u32[]{:S(2)}) collective-permute-start(bf16[288,128]{1,0:T(8,128)(2,1)S(1)} %get-tuple-element.37), channel_id=1, source_target_pairs={{0,2},{1,765},{2,760},{3,755},{4,744},{5,739},{6,8},{7,3},{8,766},... | collective-permute-start | bytes 221192 | tf_op jit(solution)/shard_map/ppermute | solution.py:85
  111.5 13.0 %collective-permute-start.6 = (bf16[288,128]{1,0:T(8,128)(2,1)S(1)}, bf16[288,128]{1,0:T(8,128)(2,1)S(1)}, u32[]{:S(2)}, u32[]{:S(2)}) collective-permute-start(bf16[288,128]{1,0:T(8,128)(2,1)S(1)} %get-tuple-element.38), channel_id=1, source_target_pairs={{0,4},{1,767},{2,756},{3,751},{4,746},{5,741},{6,10},{7,5},{8,762}... | collective-permute-start | bytes 221192 | tf_op jit(solution)/shard_map/ppermute | solution.py:85
  115.8 14.1 %collective-permute-start.4 = (bf16[192,128]{1,0:T(8,128)(2,1)S(1)}, bf16[192,128]{1,0:T(8,128)(2,1)S(1)}, u32[]{:S(2)}, u32[]{:S(2)}) collective-permute-start(bf16[192,128]{1,0:T(8,128)(2,1)S(1)} %get-tuple-element.36), channel_id=1, source_target_pairs={{0,0},{1,763},{2,758},{3,753},{4,748},{5,743},{6,6},{7,1},{8,764},... | collective-permute-start | bytes 147464 | tf_op jit(solution)/shard_map/ppermute | solution.py:85
  124.5 6.3 %collective-permute-start.7 = (f32[3,48,128]{2,1,0:T(8,128)S(1)}, f32[3,48,128]{2,1,0:T(8,128)S(1)}, u32[]{:S(2)}, u32[]{:S(2)}) collective-permute-start(f32[3,48,128]{2,1,0:T(8,128)S(1)} %pad_maximum_fusion.6), channel_id=1, source_target_pairs={{0,1},{1,0},{2,3},{3,2},{4,5},{5,4},{6,7},{7,6},{8,9},{9,8},{10,11... | collective-permute-start | bytes 221192 | tf_op jit(solution)/shard_map/ppermute | solution.py:88
